TPU v7x, 512 devices: a whole 4x8x8 slice. The times are simulated.
512 devices in a mesh: tensor: 8 (over z), expert: 64 (over y, x, core).
Axes of the slice: x: 4, y: 8, z: 8, core: 2. Of those that a mesh axis runs over, the one named last changes fastest.
Arguments:
- tokens: bfloat16 [6144, 2560], P(('expert', 'tensor')), may hold values from -6 to 6
- out_grad: bfloat16 [6144, 2560], P(('expert', 'tensor')), may hold values from -6 to 6
- expert_ids: int32 [6144, 6], P(('expert', 'tensor')), may hold values from 0 to 127, as said below
- gate_values: bfloat16 [6144, 6], P(('expert', 'tensor')), may hold values from 0.049804688 to 0.3984375
- gate_weight: bfloat16 [128, 768, 2560], P('expert', 'tensor'), may hold values from -0.125 to 0.125
- up_weight: bfloat16 [128, 768, 2560], P('expert', 'tensor'), may hold values from -0.0625 to 0.0625
- down_weight: bfloat16 [128, 768, 2560], P('expert', 'tensor'), may hold values from -0.109375 to 0.109375
Outputs:
- input_grad: bfloat16 [6144, 2560], P(('expert', 'tensor'))
Inputs may be any that keep to these rules, and one draw needn't show every extreme that they name: `expert_ids`: rows form aligned groups of 96 (the tokens of one index of the expert axis). Each row names 6 different experts on five devices of the expert axis, two of them on one device. Within a group, at most 10 rows name experts of one device, and some devices are named by exactly 10 rows.
All inputs are finite; a program needn't handle non-finite values.
Results may differ from a plain program's by a relative error of at most 0.017.
Values may be sent and summed in bfloat16 or wider, within the bound.
No kernel may reach another device: no remote copies, remote signals or barrier semaphores. Data moves between devices by JAX's collectives and lax.ppermute only.
A program may use at most 128 MiB of HBM per device.

v0:
```python
import jax
import jax.numpy as jnp
from jax import lax
from jax.sharding import PartitionSpec as P


def route_tables(group_ids, group_gates, dest_count, capacity, pair_size):
    row_count = group_ids.shape[0]
    dest_ids = group_ids // pair_size
    member = jnp.max(
        (dest_ids[:, :, None] == jnp.arange(dest_count)[None, None, :]).astype(jnp.int32), axis=1
    )
    earlier = jnp.cumsum(member, axis=0) - member
    slot_mask = (earlier[:, :, None] == jnp.arange(capacity)[None, None, :]) & (
        member[:, :, None] > 0
    )
    filled = jnp.max(slot_mask.astype(jnp.int32), axis=0)
    source = jnp.sum(
        jnp.where(slot_mask, jnp.arange(row_count)[:, None, None], 0), axis=0
    ) + row_count * (1 - filled)
    expert_hit = group_ids[:, :, None] == jnp.arange(dest_count * pair_size)[None, None, :]
    weight = jnp.sum(
        jnp.where(expert_hit, group_gates.astype(jnp.float32)[:, :, None], 0.0), axis=1
    )
    weight = weight.reshape(row_count, dest_count, pair_size)
    slot_gate = jnp.sum(jnp.where(slot_mask[:, :, :, None], weight[:, :, None, :], 0.0), axis=0)
    return (slot_mask, source, slot_gate.astype(jnp.bfloat16), member, earlier)


def pick_rows(values, source):
    padded = jnp.concatenate([values, jnp.zeros((1, values.shape[1]), values.dtype)], axis=0)
    return jnp.take(padded, source, axis=0)


def expert_terms(row_x, row_dy, row_gate, gate_weight, up_weight, down_weight):
    gate_pre = jnp.einsum("rf,ehf->erh", row_x, gate_weight, preferred_element_type=jnp.float32)
    up_pre = jnp.einsum("rf,ehf->erh", row_x, up_weight, preferred_element_type=jnp.float32)
    back_proj = jnp.einsum("rf,ehf->erh", row_dy, down_weight, preferred_element_type=jnp.float32)
    sigmoid_gate = jax.nn.sigmoid(gate_pre)
    scaled = back_proj * jnp.transpose(row_gate.astype(jnp.float32))[:, :, None]
    up_grad = (scaled * gate_pre * sigmoid_gate).astype(jnp.bfloat16)
    gate_grad = (scaled * up_pre * sigmoid_gate * (1.0 + gate_pre * (1.0 - sigmoid_gate))).astype(
        jnp.bfloat16
    )
    part_sum = jnp.einsum("erh,ehf->rf", gate_grad, gate_weight, preferred_element_type=jnp.float32)
    return part_sum + jnp.einsum(
        "erh,ehf->rf", up_grad, up_weight, preferred_element_type=jnp.float32
    )


def per_device(tokens, out_grad, expert_ids, gate_values, gate_weight, up_weight, down_weight):
    pair_size = gate_weight.shape[0]
    feature_width = tokens.shape[1]
    dest_count = lax.axis_size("expert")
    group_ids = lax.all_gather(expert_ids, "tensor", axis=0, tiled=True)
    group_rows = group_ids.shape[0]
    used_count = max(5, dest_count - dest_count // 4)
    capacity = (5 * group_rows + used_count - 1) // used_count
    group_x, group_dy, group_gates = (
        lax.all_gather(tokens, "tensor", axis=0, tiled=True),
        lax.all_gather(out_grad, "tensor", axis=0, tiled=True),
        lax.all_gather(gate_values, "tensor", axis=0, tiled=True),
    )
    slot_mask, source, slot_gate, member, earlier = route_tables(
        group_ids, group_gates, dest_count, capacity, pair_size
    )
    send_x = pick_rows(group_x, source)
    send_dy = pick_rows(group_dy, source)
    recv_x, recv_dy, recv_gate = (
        lax.all_to_all(send_x, "expert", split_axis=0, concat_axis=0, tiled=True),
        lax.all_to_all(send_dy, "expert", split_axis=0, concat_axis=0, tiled=True),
        lax.all_to_all(slot_gate, "expert", split_axis=0, concat_axis=0, tiled=True),
    )
    flat_rows = dest_count * capacity
    part_sum = expert_terms(
        recv_x.reshape(flat_rows, feature_width),
        recv_dy.reshape(flat_rows, feature_width),
        recv_gate.reshape(flat_rows, pair_size),
        gate_weight,
        up_weight,
        down_weight,
    )
    rounded = part_sum.astype(jnp.bfloat16).reshape(dest_count, capacity, feature_width)
    back_rows = lax.all_to_all(rounded, "expert", split_axis=0, concat_axis=0, tiled=True)
    group_grad = jnp.einsum(
        "gnc,ncf->gf", slot_mask.astype(jnp.bfloat16), back_rows, preferred_element_type=jnp.float32
    )
    token_grad = lax.psum_scatter(
        group_grad.astype(jnp.bfloat16), "tensor", scatter_dimension=0, tiled=True
    )
    return token_grad


def solution(mesh):
    return jax.shard_map(
        per_device,
        mesh=mesh,
        in_specs=(
            P(("expert", "tensor"), None),
            P(("expert", "tensor"), None),
            P(("expert", "tensor"), None),
            P(("expert", "tensor"), None),
            P("expert", "tensor", None),
            P("expert", "tensor", None),
            P("expert", "tensor", None),
        ),
        out_specs=P(("expert", "tensor"), None),
        check_vma=False,
    )
```

profile of v0, /device:TPU:1, one launch (start us, length us, event | category | flops | bytes accessed | tf_op | source)
XLA Modules:
  0.0 586.7 jit_solution(2470527729943489563)
XLA Ops:
  0.0 25.5 %all-gather = s32[8,12,6]{1,2,0:T(8,128)S(1)} all-gather(s32[1,12,6]{1,2,0:T(8,128)} %bitcast.55), channel_id=1, replica_groups=mesh['tensor'=8,'expert'=64] {'tensor'}, dimensions={0}, use_global_device_ids=true | all-gather | bytes 2592 | tf_op jit(solution)/shard_map/all_gather | solution.py:55
  26.0 15.6 %all-gather.2 = bf16[8,12,6]{1,2,0:T(8,128)(2,1)S(1)} all-gather(bf16[1,12,6]{1,2,0:T(8,128)(2,1)} %bitcast.56), channel_id=1, replica_groups=mesh['tensor'=8,'expert'=64] {'tensor'}, dimensions={0}, use_global_device_ids=true | all-gather | bytes 1296 | tf_op jit(solution)/shard_map/all_gather | solution.py:62
  43.1 22.6 %all-to-all-start.1 = ((bf16[64,10,2]{1,2,0:T(2,128)(2,1)}), bf16[64,10,2]{1,2,0:T(2,128)(2,1)S(1)}, u32[]{:S(2)}, u32[]{:S(2)}) async-start(bf16[64,10,2]{1,2,0:T(2,128)(2,1)} %copy.60), calls=%async_computation.1 | async-start | bytes 65536 | tf_op jit(solution)/shard_map/all_to_all | solution.py:72
  66.4 21.0 %all-gather.1 = bf16[8,12,2560]{2,1,0:T(8,128)(2,1)S(1)} all-gather(bf16[1,12,2560]{2,1,0:T(8,128)(2,1)} %bitcast.52), channel_id=1, replica_groups=mesh['tensor'=8,'expert'=64] {'tensor'}, dimensions={0}, use_global_device_ids=true | all-gather | bytes 552960 | tf_op jit(solution)/shard_map/all_gather | solution.py:61
  87.5 4.4 gather_fusion
  91.9 6.9 %reshape.75 = bf16[64,10,2560]{2,1,0:T(8,128)(2,1)} reshape(bf16[640,2560]{1,0:T(8,128)(2,1)} %gather_fusion) | data formatting | bytes 6553600 | tf_op jit(solution)/shard_map/jit(_take)/gather | solution.py:32
  98.8 20.1 %all-gather.3 = bf16[8,12,2560]{2,1,0:T(8,128)(2,1)S(1)} all-gather(bf16[1,12,2560]{2,1,0:T(8,128)(2,1)S(1)} %bitcast.53), channel_id=1, replica_groups=mesh['tensor'=8,'expert'=64] {'tensor'}, dimensions={0}, use_global_device_ids=true | all-gather | bytes 552960 | tf_op jit(solution)/shard_map/all_gather | solution.py:60
  119.0 4.4 gather_fusion.1
  123.4 6.9 %reshape.79 = bf16[64,10,2560]{2,1,0:T(8,128)(2,1)} reshape(bf16[640,2560]{1,0:T(8,128)(2,1)} %gather_fusion.1) | data formatting | bytes 6553600 | tf_op jit(solution)/shard_map/jit(_take)/gather | solution.py:32
  130.4 9.0 %broadcast_select_fusion = (bf16[64,10,2560]{2,1,0:T(8,128)(2,1)}, bf16[64,10,2560]{2,1,0:T(8,128)(2,1)}) fusion(bf16[64,10,2560]{2,1,0:T(8,128)(2,1)} %reshape.79, pred[64,10]{1,0:T(8,128)(4,1)S(1)} %copy.55, bf16[64,10,2560]{2,1,0:T(8,128)(2,1)} %reshape.75), kind=kLoop, calls=%fused_computation.4 | loop fusion | flops 3276800 | bytes 13107840 | tf_op jit(solution)/shard_map/jit(_take)/select_n | solution.py:32
  139.4 138.9 %all_to_all.20 = bf16[64,10,2560]{2,1,0:T(8,128)(2,1)} all-to-all(bf16[64,10,2560]{2,1,0:T(8,128)(2,1)} %get-tuple-element.10), channel_id=1, replica_groups=mesh['tensor'=8,'expert'=64] {'expert'}, dimensions={0} | all-to-all | bytes 6553600 | tf_op jit(solution)/shard_map/all_to_all | solution.py:70
  278.3 6.8 %all-to-all-start = ((bf16[64,10,2560]{2,1,0:T(8,128)(2,1)}), bf16[64,10,2560]{2,1,0:T(8,128)(2,1)}, u32[]{:S(2)}, u32[]{:S(2)}) async-start(bf16[64,10,2560]{2,1,0:T(8,128)(2,1)} %get-tuple-element.11), calls=%async_computation | async-start | bytes 10485760 | tf_op jit(solution)/shard_map/all_to_all | solution.py:71
  285.4 7.0 %reshape.81 = bf16[640,2560,1]{1,0,2:T(8,128)(2,1)} reshape(bf16[64,10,2560]{2,1,0:T(8,128)(2,1)} %all_to_all.20) | data formatting | bytes 6553600 | tf_op jit(solution)/shard_map/reshape | solution.py:76
  292.5 3.1 convolution_bitcast_fusion.1
  295.6 105.8 %all-to-all-done = bf16[64,10,2560]{2,1,0:T(8,128)(2,1)} async-done(((bf16[64,10,2560]{2,1,0:T(8,128)(2,1)}), bf16[64,10,2560]{2,1,0:T(8,128)(2,1)}, u32[]{:S(2)}, u32[]{:S(2)}) %all-to-all-start) | async-done | bytes 3276832 | tf_op jit(solution)/shard_map/all_to_all | solution.py:71
  401.4 7.0 %reshape.80 = bf16[640,2560,1]{1,0,2:T(8,128)(2,1)} reshape(bf16[64,10,2560]{2,1,0:T(8,128)(2,1)} %all-to-all-done) | data formatting | bytes 6553600 | tf_op jit(solution)/shard_map/reshape | solution.py:77
  408.4 3.4 fusion.4
  411.8 7.3 %fusion.9 = f32[640,2560,1]{1,0,2:T(8,128)} fusion(bf16[2,96,2560]{2,1,0:T(8,128)(2,1)S(1)} %copy-done.1, f32[2,640,96]{1,2,0:T(8,128)S(1)} %fusion.4, bf16[640,2560,1]{1,0,2:T(8,128)(2,1)} %reshape.81, bf16[2,96,2560]{2,1,0:T(8,128)(2,1)S(1)} %copy-done, f32[2,640,96]{1,2,0:T(8,128)S(1)} %convolution_bitcast_fusion.1), kind=kOutput, calls=%fused_computation.17 | convolution fusion | flops 1259520000 | bytes 12779520 | tf_op jit(solution)/shard_map/erh,ehf->rf/dot_general | solution.py:45
  419.2 5.7 fusion.1
  424.8 6.8 %reshape.41 = bf16[64,10,2560]{2,1,0:T(8,128)(2,1)} reshape(bf16[640,2560]{1,0:T(8,128)(2,1)} %fusion.1) | data formatting | bytes 6553600 | tf_op jit(solution)/shard_map/reshape | solution.py:83
  431.7 125.5 %all_to_all.21 = bf16[64,10,2560]{2,1,0:T(8,128)(2,1)S(1)} all-to-all(bf16[64,10,2560]{2,1,0:T(8,128)(2,1)} %reshape.41), channel_id=1, replica_groups=mesh['tensor'=8,'expert'=64] {'expert'}, dimensions={0} | all-to-all | bytes 6553600 | tf_op jit(solution)/shard_map/all_to_all | solution.py:84
  557.2 3.7 fusion.2
  560.9 18.0 %fusion = bf16[16,2560]{1,0:T(8,128)(2,1)S(1)} fusion(bf16[96,2560]{1,0:T(8,128)(2,1)S(1)} %fusion.2), kind=kCustom, calls=%all-reduce-scatter | all-reduce-scatter fusion | flops 327681 | bytes 575488
  578.9 2.6 collective-permute-start
  (44 shorter events, 7.8 us)
Async XLA Ops:
  0.0 411.8 %copy-start = (bf16[2,96,2560]{2,1,0:T(8,128)(2,1)S(1)}, bf16[2,96,2560]{2,1,0:T(8,128)(2,1)}, u32[]{:S(2)}) copy-start(bf16[2,96,2560]{2,1,0:T(8,128)(2,1)} %param.14) | copy-start | bytes 2949124
  43.1 96.3 %all-to-all-start.1 = ((bf16[64,10,2]{1,2,0:T(2,128)(2,1)}), bf16[64,10,2]{1,2,0:T(2,128)(2,1)S(1)}, u32[]{:S(2)}, u32[]{:S(2)}) async-start(bf16[64,10,2]{1,2,0:T(2,128)(2,1)} %copy.60), calls=%async_computation.1 | async-start | bytes 65536 | tf_op jit(solution)/shard_map/all_to_all | solution.py:72
  91.9 6.9 %copy-start.2 = (bf16[12,2560]{1,0:T(8,128)(2,1)S(1)}, bf16[12,2560]{1,0:T(8,128)(2,1)}, u32[]{:S(2)}) copy-start(bf16[12,2560]{1,0:T(8,128)(2,1)} %param.9) | copy-start | bytes 184324
  278.3 123.1 %all-to-all-start = ((bf16[64,10,2560]{2,1,0:T(8,128)(2,1)}), bf16[64,10,2560]{2,1,0:T(8,128)(2,1)}, u32[]{:S(2)}, u32[]{:S(2)}) async-start(bf16[64,10,2560]{2,1,0:T(8,128)(2,1)} %get-tuple-element.11), calls=%async_computation | async-start | bytes 10485760 | tf_op jit(solution)/shard_map/all_to_all | solution.py:71
  285.1 7.4 %copy-start.1 = (bf16[2,96,2560]{2,1,0:T(8,128)(2,1)S(1)}, bf16[2,96,2560]{2,1,0:T(8,128)(2,1)}, u32[]{:S(2)}) copy-start(bf16[2,96,2560]{2,1,0:T(8,128)(2,1)} %param.13) | copy-start | bytes 2949124
  578.9 6.7 %collective-permute-start = (bf16[16,2560]{1,0:T(8,128)(2,1)S(1)}, bf16[16,2560]{1,0:T(8,128)(2,1)S(1)}, u32[]{:S(2)}, u32[]{:S(2)}) collective-permute-start(bf16[16,2560]{1,0:T(8,128)(2,1)S(1)} %fusion), channel_id=1, source_target_pairs={{0,64},{64,128},{128,192},{192,256},{256,320},{320,384},{384,448},... | collective-permute-start | bytes 245768
  581.6 4.0 collective-permute-start.1
where the time goes:
time: 593 us; the launch traced here: 587 us
  blocking collectives  365 us (62%)
  waiting for transfers between devices  106 us (18%)
  local copies, waits for them, and re-layouts  47.9 us (8%)
  starting transfers between devices  34.1 us (6%)
  matrix products  23.3 us (4%)
  other arithmetic  10.1 us (2%)
    all_to_all x1, blocking collectives, per_device(): lax.all_to_all(send_x, 'expert', split_axis=0, concat_axis=0, tiled=True)  139 us
    all_to_all x1, blocking collectives, per_device(): lax.all_to_all(rounded, 'expert', split_axis=0, concat_axis=0, tiled=True)  126 us
    all_to_all x1, waiting for transfers between devices, per_device(): lax.all_to_all(send_dy, 'expert', split_axis=0, concat_axis=0, tiled=True)  106 us
    all_gather x1, blocking collectives, per_device(): group_ids = lax.all_gather(expert_ids, 'tensor', axis=0, tiled=True)  25.5 us
    all_to_all x1, starting transfers between devices, per_device(): lax.all_to_all(slot_gate, 'expert', split_axis=0, concat_axis=0, tiled=True)  22.6 us
    gather x4, local copies, waits for them, and re-layouts, pick_rows(): return jnp.take(padded, source, axis=0)  22.5 us
    all_gather x1, blocking collectives, per_device(): lax.all_gather(out_grad, 'tensor', axis=0, tiled=True)  21 us
    all_gather x1, blocking collectives, per_device(): lax.all_gather(tokens, 'tensor', axis=0, tiled=True)  20.1 us
  transfers between devices with their start and end apart: 4, of which 1 were waited for; matrix products, arithmetic and copies ran while one was open for 8% of the time, Pallas kernels for 0%

commit v1 on v0

v1 whole, which is shorter than its diff:
```python
import jax
import jax.numpy as jnp
from jax import lax
from jax.experimental import pallas as pl
from jax.experimental.pallas import tpu as pltpu
from jax.sharding import PartitionSpec as P

BF = jnp.bfloat16
F32 = jnp.float32
I32 = jnp.int32
D = 2560
OWN = 12
PADDED = 16
NT = 8
NE = 64
NTOK = NT * PADDED
ROWS = NE * 8
HID2 = 192
FA = 1024
FB = (D - FA) // 4
RA = 512
RB = (D - RA) // NT
VMEM = pl.BlockSpec(memory_space=pltpu.VMEM)
LIMIT = 56 * 1024 * 1024


def call(kernel, out_shapes, name, flops=0, moved=0, scratch=()):
    return pl.pallas_call(
        kernel,
        out_shape=out_shapes,
        scratch_shapes=scratch,
        name=name,
        cost_estimate=pl.CostEstimate(flops=flops, bytes_accessed=moved, transcendentals=0),
        compiler_params=pltpu.CompilerParams(vmem_limit_bytes=LIMIT),
    )


def dot(a, b):
    return jnp.dot(a, b, preferred_element_type=F32)


def dot_t(a, b):
    return lax.dot_general(a, b, (((1,), (1,)), ((), ())), preferred_element_type=F32)


def iota(shape, dim):
    return lax.broadcasted_iota(I32, shape, dim)


def start_kernel(x_ref, dy_ref, meta_ref, msg_ref, all_ref):
    msg_ref[...] = jnp.zeros_like(msg_ref)
    all_ref[...] = jnp.zeros_like(all_ref)
    all_ref[0:OWN, 0:D] = x_ref[...]
    all_ref[0:OWN, D : 2 * D] = dy_ref[...]
    for t in range(NT):
        src = x_ref if t < 4 else dy_ref
        low = FA + FB * (t % 4)
        msg_ref[t, 0:OWN, 0:FB] = src[:, low : low + FB]
        msg_ref[t, 0:OWN, FB : FB + 128] = meta_ref[...]


def positions(meta):
    ids = meta.astype(F32).astype(I32)
    lane = iota((NTOK, 128), 1)
    row = iota((NTOK, 128), 0)
    hit = jnp.zeros((NTOK, 128), jnp.bool_)
    for k in range(6):
        hit = hit | ((ids[:, k : k + 1] >> 1) == (lane >> 1))
    member = jnp.where(hit & ((row & 15) < OWN), 1.0, 0.0)
    lower = jnp.where(lane < row, 1.0, 0.0).astype(BF)
    earlier = dot(lower, member.astype(BF))
    return jnp.where(member > 0.5, earlier, -1.0), ids


def one_hots(pos):
    row = iota((ROWS, 128), 0)
    lane = iota((ROWS, 128), 1)
    pick = jnp.where(lane == 2 * (row >> 3), 1.0, 0.0).astype(BF)
    spread = dot_t(pick, pos.astype(BF)).astype(I32)
    sub = row & 7
    main = jnp.where(spread == sub, 1.0, 0.0).astype(BF)
    left = jnp.where(spread == 8 + (sub >> 2), 1.0, 0.0).astype(BF)
    return main, left


def fold(left_rows, tiles, first, sub4):
    out = jnp.zeros((ROWS, 128), F32)
    for k in range(tiles):
        low = 128 * (first + k)
        out = jnp.where(sub4 == k, left_rows[:, low : low + 128], out)
    return out


def pack_b_kernel(msg_ref, out_ref):
    meta = msg_ref[:, FB : FB + 128]
    pos, ids = positions(meta)
    main, left = one_hots(pos)
    values = msg_ref[:, 0:FB]
    out_ref[:, 0:FB] = dot(main, values).astype(BF)
    gates = meta.astype(F32)
    lane = iota((NTOK, 128), 1)
    weight = jnp.zeros((NTOK, 128), F32)
    for k in range(6):
        weight = weight + jnp.where(ids[:, k : k + 1] == lane, gates[:, 6 + k : 7 + k], 0.0)
    weight = weight.astype(BF)
    row16 = iota((16, 128), 0)
    gate_of = jnp.zeros((16, 128), F32)
    for s in range(10):
        col = jnp.sum(jnp.where(pos == float(s), weight.astype(F32), 0.0), axis=0, keepdims=True)
        gate_of = jnp.where(row16 == s, col, gate_of)
    gate_of = jnp.concatenate([gate_of, jnp.zeros((112, 128), F32)], axis=0).astype(BF)
    row = iota((ROWS, 128), 0)
    sub = row & 7
    wide = iota((ROWS, 128), 1)
    pick = jnp.where((wide == 2 * (row >> 3) + (sub >> 2)) & ((sub & 3) == 3), 1.0, 0.0)
    gate_tile = dot_t(pick.astype(BF), gate_of)
    folded = fold(dot(left, values), 3, 0, sub & 3)
    out_ref[:, FB : FB + 128] = jnp.where((sub & 3) == 3, gate_tile, folded).astype(BF)


def pack_a_kernel(msg_ref, x_ref, out_ref):
    pos, _ = positions(msg_ref[:, FB : FB + 128])
    main, left = one_hots(pos)
    sub4 = iota((ROWS, 128), 0) & 3
    for part in range(2):
        values = x_ref[:, part * D : part * D + FA]
        out_ref[:, part * FA : (part + 1) * FA] = dot(main, values).astype(BF)
        spread = dot(left, values)
        for q in range(2):
            low = 2 * FA + (2 * part + q) * 128
            out_ref[:, low : low + 128] = fold(spread, 4, 4 * q, sub4).astype(BF)


def perm(inverse):
    row = iota((ROWS, ROWS), 0)
    col = iota((ROWS, ROWS), 1)
    if inverse:
        row, col = col, row
    return jnp.where(((col & 7) == (row >> 6)) & ((col >> 3) == (row & 63)), 1.0, 0.0).astype(BF)


def compute_kernel(b_ref, a_ref, wg_ref, wu_ref, wd_ref, rs_ref, back_ref, left_ref, z_ref):
    turn = perm(False)
    for q in range(4):
        tile = dot(turn, a_ref[:, 2 * FA + 128 * q : 2 * FA + 128 * (q + 1)]).astype(BF)
        base = (q // 2) * D + (q % 2) * 512
        for s in range(2):
            for k in range(4):
                left_ref[64 * s : 64 * s + 64, base + 128 * k : base + 128 * (k + 1)] = tile[
                    64 * (4 * s + k) : 64 * (4 * s + k + 1)
                ]
    gate_tiles = None
    for t in range(NT):
        tile = dot(turn, b_ref[ROWS * t : ROWS * (t + 1), FB : FB + 128]).astype(BF)
        base = (t // 4) * D + FA + (t % 4) * FB
        if t == 0:
            gate_tiles = (tile[64 * 3 : 64 * 4], tile[64 * 7 : 64 * 8])
        for s in range(2):
            for k in range(3):
                left_ref[64 * s : 64 * s + 64, base + 128 * k : base + 128 * (k + 1)] = tile[
                    64 * (4 * s + k) : 64 * (4 * s + k + 1)
                ]
    wg = wg_ref[...].reshape(HID2, D)
    wu = wu_ref[...].reshape(HID2, D)
    wd = wd_ref[...].reshape(HID2, D)
    row = iota((ROWS, 64), 0)
    spread = jnp.where((row >> 3) == iota((ROWS, 64), 1), 1.0, 0.0).astype(BF)
    wide = iota((ROWS, 128), 1)
    sub = iota((ROWS, 128), 0) & 7
    gate_main = []
    gate_left = []
    for e in range(2):
        both = dot(spread, gate_tiles[e])
        gate_main.append(jnp.sum(jnp.where(wide == sub, both, 0.0), axis=1, keepdims=True))
        own = gate_tiles[e].astype(F32)
        gate_left.append(jnp.concatenate([own[:, 8:9], own[:, 9:10]], axis=0))

    def grads(gate_pre, up_pre, back_proj, gates):
        lane = iota(gate_pre.shape, 1)
        scaled = back_proj * jnp.where(lane < HID2 // 2, gates[0], gates[1])
        sig = 1.0 / (1.0 + jnp.exp(-gate_pre))
        up_grad = (scaled * gate_pre * sig).astype(BF)
        gate_grad = (scaled * up_pre * sig * (1.0 + gate_pre * (1.0 - sig))).astype(BF)
        return gate_grad, up_grad

    gate_pre = dot_t(a_ref[:, 0:FA], wg[:, 0:FA])
    up_pre = dot_t(a_ref[:, 0:FA], wu[:, 0:FA])
    back_proj = dot_t(a_ref[:, FA : 2 * FA], wd[:, 0:FA])
    for t in range(4):
        low = FA + FB * t
        rows = b_ref[ROWS * t : ROWS * (t + 1), 0:FB]
        gate_pre = gate_pre + dot_t(rows, wg[:, low : low + FB])
        up_pre = up_pre + dot_t(rows, wu[:, low : low + FB])
        rows = b_ref[ROWS * (t + 4) : ROWS * (t + 5), 0:FB]
        back_proj = back_proj + dot_t(rows, wd[:, low : low + FB])
    gate_grad, up_grad = grads(gate_pre, up_pre, back_proj, gate_main)
    gate_grad_l, up_grad_l = grads(
        dot_t(left_ref[:, 0:D], wg),
        dot_t(left_ref[:, 0:D], wu),
        dot_t(left_ref[:, D : 2 * D], wd),
        gate_left,
    )
    turn_back = perm(True)
    z_ref[...] = jnp.zeros_like(z_ref)
    for t in range(NT + 1):
        low = 0 if t == NT else RA + RB * t
        width = RA if t == NT else RB
        part = dot(gate_grad, wg[:, low : low + width]) + dot(up_grad, wu[:, low : low + width])
        part_l = dot(gate_grad_l, wg[:, low : low + width]) + dot(up_grad_l, wu[:, low : low + width])
        part_l = part_l.astype(BF)
        for s in range(2):
            for k in range(width // 128):
                z_ref[64 * (4 * s + k) : 64 * (4 * s + k + 1), :] = part_l[
                    64 * s : 64 * s + 64, 128 * k : 128 * (k + 1)
                ]
        folded = dot(turn_back, z_ref[...]).astype(BF)
        if t == NT:
            back_ref[:, 0:RA] = part.astype(BF)
            back_ref[:, RA : RA + 128] = folded
        else:
            rs_ref[t, :, 0:RB] = part.astype(BF)
            rs_ref[t, :, RB : RB + 128] = folded


def combine_kernel(msg_ref, b_ref, a_ref, out_ref):
    pos, _ = positions(msg_ref[:, FB : FB + 128])
    row = iota((128, ROWS), 0)
    col = iota((128, ROWS), 1)
    pick = jnp.where(row == 2 * (col >> 3), 1.0, 0.0).astype(BF)
    spread = dot(pos.astype(BF), pick).astype(I32)
    sub = col & 7
    main = jnp.where(spread == sub, 1.0, 0.0).astype(BF)
    left = spread == 8 + (sub >> 2)
    for k in range(4):
        left_k = jnp.where(left & ((sub & 3) == k), 1.0, 0.0).astype(BF)
        cols = slice(128 * k, 128 * (k + 1))
        total = dot(main, a_ref[:, cols]) + dot(left_k, a_ref[:, RA : RA + 128])
        out_ref[:, cols] = total.astype(BF)
        if k < 2:
            total = dot(main, b_ref[:, cols]) + dot(left_k, b_ref[:, RB : RB + 128])
            out_ref[:, RA + 128 * k : RA + 128 * (k + 1)] = total.astype(BF)


def finish_kernel(in_ref, out_ref):
    total = in_ref[0, :, 0:RA].astype(F32)
    for t in range(1, NT):
        total = total + in_ref[t, :, 0:RA].astype(F32)
    out_ref[:, 0:RA] = total.astype(BF)[0:OWN]
    for t in range(NT):
        low = RA + RB * t
        out_ref[:, low : low + RB] = in_ref[t, 0:OWN, RA : RA + RB]


def per_device(tokens, out_grad, expert_ids, gate_values, gate_weight, up_weight, down_weight):
    meta = jnp.concatenate([expert_ids.astype(BF), gate_values], axis=1)
    meta = jnp.pad(meta, ((0, 0), (0, 128 - meta.shape[1])))
    msg, both = call(
        start_kernel,
        (
            jax.ShapeDtypeStruct((NT, PADDED, FB + 128), BF),
            jax.ShapeDtypeStruct((PADDED, 2 * D), BF),
        ),
        "start",
    )(tokens, out_grad, meta)
    both_all = lax.all_gather(both, "tensor", axis=0, tiled=True)
    msg = lax.all_to_all(msg, "tensor", 0, 0, tiled=True).reshape(NTOK, FB + 128)
    send_b = call(
        pack_b_kernel, jax.ShapeDtypeStruct((ROWS, FB + 128), BF), "pack_b", flops=2 * ROWS * 128 * 1024
    )(msg)
    recv_b = lax.all_to_all(send_b.reshape(NE, 8, FB + 128), "expert", 0, 0, tiled=True)
    all_b = lax.all_gather(recv_b.reshape(ROWS, FB + 128), "tensor", axis=0, tiled=True)
    send_a = call(
        pack_a_kernel,
        jax.ShapeDtypeStruct((ROWS, 2 * FA + 512), BF),
        "pack_a",
        flops=2 * ROWS * 128 * 4096,
    )(msg, both_all)
    recv_a = lax.all_to_all(send_a.reshape(NE, 8, 2 * FA + 512), "expert", 0, 0, tiled=True)
    to_sum, to_send = call(
        compute_kernel,
        (
            jax.ShapeDtypeStruct((NT, ROWS, RB + 128), BF),
            jax.ShapeDtypeStruct((ROWS, RA + 128), BF),
        ),
        "experts",
        flops=10 * 640 * D * HID2,
        moved=16_000_000,
        scratch=[pltpu.VMEM((128, 2 * D), BF), pltpu.VMEM((ROWS, 128), BF)],
    )(all_b, recv_a.reshape(ROWS, 2 * FA + 512), gate_weight, up_weight, down_weight)
    summed = lax.psum_scatter(to_sum, "tensor", scatter_dimension=0, tiled=False)
    back_a = lax.all_to_all(to_send.reshape(NE, 8, RA + 128), "expert", 0, 0, tiled=True)
    back_b = lax.all_to_all(summed.reshape(NE, 8, RB + 128), "expert", 0, 0, tiled=True)
    last = call(
        combine_kernel,
        jax.ShapeDtypeStruct((NTOK, RA + RB), BF),
        "combine",
        flops=2 * ROWS * 128 * 1536,
    )(msg, back_b.reshape(ROWS, RB + 128), back_a.reshape(ROWS, RA + 128))
    last = lax.all_to_all(last.reshape(NT, PADDED, RA + RB), "tensor", 0, 0, tiled=True)
    return call(finish_kernel, jax.ShapeDtypeStruct((OWN, D), BF), "finish")(last)


def solution(mesh):
    return jax.shard_map(
        per_device,
        mesh=mesh,
        in_specs=(
            P(("expert", "tensor"), None),
            P(("expert", "tensor"), None),
            P(("expert", "tensor"), None),
            P(("expert", "tensor"), None),
            P("expert", "tensor", None),
            P("expert", "tensor", None),
            P("expert", "tensor", None),
        ),
        out_specs=P(("expert", "tensor"), None),
        check_vma=False,
    )
```

time: 593 us -> 247 us (0.42)
  blocking collectives: 365 us -> 187 us
  waiting for transfers between devices: 106 us -> 14.2 us
  local copies, waits for them, and re-layouts: 47.9 us -> 1.94 us
  starting transfers between devices: 34.1 us -> 0.09 us
  Pallas kernels: 0 us -> 28.5 us
  matrix products: 23.3 us -> 0 us
  between operations: 0.89 us -> 13.1 us
  other arithmetic: 10.1 us -> 1.38 us
    all_to_all x2 -> x0, waiting for transfers between devices: 106 us -> none  [the longest x1 106 us: per_device(): lax.all_to_all(send_dy, 'expert', split_axis=0, concat_axis=0, tiled=True)]
    all_gather x4 -> x0, blocking collectives: 82.2 us -> none  [the longest x1 25.5 us: per_device(): group_ids = lax.all_gather(expert_ids, 'tensor', axis=0, tiled=True)]
    all_to_all x2 -> x6, blocking collectives: 264 us -> 187 us  [the longest x1 69.9 us: per_device(): lax.all_to_all(send_a.reshape(NE, 8, 2 * FA + 512), 'expert', 0, 0, tiled...]
    all_to_all x2 -> x0, starting transfers between devices: 29.4 us -> none  [the longest x1 22.6 us: per_device(): lax.all_to_all(slot_gate, 'expert', split_axis=0, concat_axis=0, tiled=True)]
    pallas_call x0 -> x6, Pallas kernels: none -> 28.5 us  [the longest x1 14.8 us: per_device(): call(compute_kernel, (jax.ShapeDtypeStruct((NT, ROWS, RB + 128), BF), jax...]
    dot_general x5 -> x0, matrix products: 23.3 us -> none  [the longest x1 7.34 us: expert_terms(): jnp.einsum('erh,ehf->rf', gate_grad, gate_weight, preferred_element_type=...]
    gather x4 -> x0, local copies, waits for them, and re-layouts: 22.5 us -> none  [pick_rows(): return jnp.take(padded, source, axis=0)]
    reshape x3 -> x0, local copies, waits for them, and re-layouts: 20.9 us -> none  [the longest x1 7.02 us: per_device(): recv_x.reshape(flat_rows, feature_width)]
  transfers between devices with their start and end apart: 4 -> 3, of which waited for: 1 -> 1; matrix products, arithmetic and copies ran while one was open for 8% -> 0% of each run, Pallas kernels for 0% -> 3%
where the time goes in v1:
time: 247 us; the launch traced here: 246 us
  blocking collectives  187 us (76%)
  Pallas kernels  28.5 us (12%)
  waiting for transfers between devices  14.2 us (6%)
  between operations  13.1 us (5%)
    all_to_all x1, blocking collectives, per_device(): lax.all_to_all(send_a.reshape(NE, 8, 2 * FA + 512), 'expert', 0, 0, tiled...  69.9 us
    all_to_all x1, blocking collectives, per_device(): lax.all_to_all(send_b.reshape(NE, 8, FB + 128), 'expert', 0, 0, tiled=True)  30.2 us
    all_to_all x1, blocking collectives, per_device(): lax.all_to_all(summed.reshape(NE, 8, RB + 128), 'expert', 0, 0, tiled=True)  27.9 us
    all_to_all x1, blocking collectives, per_device(): lax.all_to_all(to_send.reshape(NE, 8, RA + 128), 'expert', 0, 0, tiled=True)  25.9 us
    all_to_all x1, blocking collectives, per_device(): lax.all_to_all(msg, 'tensor', 0, 0, tiled=True).reshape(NTOK, FB + 128)  18.7 us
    pallas_call x1, Pallas kernels, per_device(): call(compute_kernel, (jax.ShapeDtypeStruct((NT, ROWS, RB + 128), BF), jax...  14.8 us
    all_to_all x1, blocking collectives, per_device(): lax.all_to_all(last.reshape(NT, PADDED, RA + RB), 'tensor', 0, 0, tiled=T...  14.2 us
    reduce_scatter x1, waiting for transfers between devices, per_device(): lax.psum_scatter(to_sum, 'tensor', scatter_dimension=0, tiled=False)  14.1 us
  transfers between devices with their start and end apart: 3, of which 1 were waited for; matrix products, arithmetic and copies ran while one was open for 0% of the time, Pallas kernels for 3%

profile of v1, /device:TPU:1, one launch (start us, length us, event | category | flops | bytes accessed | tf_op | source)
XLA Modules:
  0.0 246.1 jit_solution(11438660862671716734)
XLA Ops:
  6.5 0.7 convert_element_type.5
  7.2 0.1 copy.10
  7.3 0.8 copy.11
  8.1 0.7 fusion.2.meta_ref
  8.8 1.7 start.1
  10.5 0.0 all-gather.5.cloned.1.call-update
  10.5 0.0 all-gather.3.cloned.1.call-start
  10.6 18.7 %all_to_all.30 = bf16[8,16,512]{2,1,0:T(8,128)(2,1)} all-to-all(bf16[8,16,512]{2,1,0:T(8,128)(2,1)} %get-tuple-element.9), channel_id=1, replica_groups=mesh['tensor'=8,'expert'=64] {'tensor'}, dimensions={0} | all-to-all | bytes 262144 | tf_op jit(solution)/shard_map/all_to_all | solution.py:266
  29.3 2.7 %pack_b.1 = bf16[512,512]{1,0:T(8,128)(2,1)} custom-call(bf16[128,512]{1,0:T(8,128)(2,1)} %bitcast.15), custom_call_target="tpu_custom_call" | custom-call | flops 134217728 | tf_op jit(solution)/shard_map/pack_b/pallas_call | solution.py:267
  32.0 30.2 %all_to_all.31 = bf16[64,8,512]{2,1,0:T(8,128)(2,1)} all-to-all(bf16[64,8,512]{2,1,0:T(8,128)(2,1)} %bitcast.13), channel_id=1, replica_groups=mesh['tensor'=8,'expert'=64] {'expert'}, dimensions={0} | all-to-all | bytes 1048576 | tf_op jit(solution)/shard_map/all_to_all | solution.py:270
  62.2 0.0 all-gather.3.cloned.1.call-update
  62.2 0.0 reduce-scatter.2.cloned.1.call-start
  62.3 0.0 all-gather.5.cloned.1.call-done.x_ref
  62.3 4.7 %pack_a.1 = bf16[512,2560]{1,0:T(8,128)(2,1)} custom-call(bf16[128,512]{1,0:T(8,128)(2,1)} %bitcast.16, bf16[128,5120]{1,0:T(8,128)(2,1)} %all-gather.5.cloned.1.call-done.x_ref), custom_call_target="tpu_custom_call" | custom-call | flops 536870912 | tf_op jit(solution)/shard_map/pack_a/pallas_call | solution.py:272
  67.0 69.9 %all_to_all.32 = bf16[64,8,2560]{2,1,0:T(8,128)(2,1)} all-to-all(bf16[64,8,2560]{2,1,0:T(8,128)(2,1)} %bitcast.10), channel_id=1, replica_groups=mesh['tensor'=8,'expert'=64] {'expert'}, dimensions={0} | all-to-all | bytes 5242880 | tf_op jit(solution)/shard_map/all_to_all | solution.py:278
  136.9 14.8 %experts.1 = (bf16[8,512,384]{2,1,0:T(8,128)(2,1)}, bf16[512,640]{1,0:T(8,128)(2,1)}) custom-call(bf16[4096,512]{1,0:T(8,128)(2,1)} %all-gather.3.cloned.1.call-done.b_ref, bf16[512,2560]{1,0:T(8,128)(2,1)} %bitcast.11, bf16[2,96,2560]{2,1,0:T(8,128)(2,1)} %wg_ref.1, bf16[2,96,2560]{2,1,0:T(8,128)(2,1)} %wu_ref.1, bf16[2,96,2560]{2,1,0:T(8,128)(2,1)} %wd_ref.1), custom_call_target="tpu_custom_call" | custom-call | flops 3145728000 | bytes 16000000 | tf_op jit(solution)/shard_map/experts/pallas_call | solution.py:279
  151.8 0.0 reduce-scatter.2.cloned.1.call-update
  151.8 1.1 copy-done
  152.9 25.9 %all_to_all.33 = bf16[64,8,640]{2,1,0:T(8,128)(2,1)} all-to-all(bf16[64,8,640]{2,1,0:T(8,128)(2,1)S(1)} %bitcast.20), channel_id=1, replica_groups=mesh['tensor'=8,'expert'=64] {'expert'}, dimensions={0} | all-to-all | bytes 1310720 | tf_op jit(solution)/shard_map/all_to_all | solution.py:291
  178.8 14.1 %reduce-scatter.2.cloned.1.call-done = bf16[1,512,384]{2,1,0:T(8,128)(2,1)} async-done(((bf16[8,512,384]{2,1,0:T(8,128)(2,1)}), bf16[1,512,384]{2,1,0:T(8,128)(2,1)}) %reduce-scatter.2.cloned.1.call-update) | async-done | bytes 393232 | tf_op jit(solution)/shard_map/reduce_scatter | solution.py:290
  192.9 27.9 %all_to_all.34 = bf16[64,8,384]{2,1,0:T(8,128)(2,1)} all-to-all(bf16[64,8,384]{2,1,0:T(8,128)(2,1)} %bitcast.21), channel_id=1, replica_groups=mesh['tensor'=8,'expert'=64] {'expert'}, dimensions={0} | all-to-all | bytes 786432 | tf_op jit(solution)/shard_map/all_to_all | solution.py:292
  220.8 3.0 %combine.1 = bf16[128,768]{1,0:T(8,128)(2,1)} custom-call(bf16[128,512]{1,0:T(8,128)(2,1)} %bitcast.17, bf16[512,384]{1,0:T(8,128)(2,1)} %bitcast.18, bf16[512,640]{1,0:T(8,128)(2,1)} %bitcast.12), custom_call_target="tpu_custom_call" | custom-call | flops 201326592 | tf_op jit(solution)/shard_map/combine/pallas_call | solution.py:293
  223.8 14.2 %all_to_all.35.in_ref = bf16[8,16,768]{2,1,0:T(8,128)(2,1)} all-to-all(bf16[8,16,768]{2,1,0:T(8,128)(2,1)} %bitcast.19), channel_id=1, replica_groups=mesh['tensor'=8,'expert'=64] {'tensor'}, dimensions={0} | all-to-all | bytes 393216 | tf_op jit(solution)/shard_map/all_to_all | solution.py:299
  238.0 1.6 finish.1
  (3 shorter events, 0.0 us)
Async XLA Ops:
  6.5 55.8 %all-gather.5.cloned.1.call-start = ((), (), s32[]{:S(2)}) async-start(), calls=%async_computation.8 | async-start | bytes 1474560 | tf_op jit(solution)/shard_map/all_gather | solution.py:265
  10.5 126.4 %all-gather.3.cloned.1.call-start = ((), (), s32[]{:S(2)}) async-start(), calls=%async_computation.7 | async-start | bytes 4718592 | tf_op jit(solution)/shard_map/all_gather | solution.py:271
  62.2 130.7 %reduce-scatter.2.cloned.1.call-start = ((), (), s32[]{:S(2)}) async-start(), calls=%async_computation.9 | async-start | bytes 3538944 | tf_op jit(solution)/shard_map/reduce_scatter | solution.py:290
  151.8 1.1 copy-start
Sparse Core Ops, SparseCore 0:
  10.6 43.7 all-gather.4
  62.4 54.9 all-gather.2
  151.9 40.9 reduce-scatter.1

commit v2 on v0

v2 whole, which is shorter than its diff:
```python
import jax
import jax.numpy as jnp
from jax import lax
from jax.experimental import pallas as pl
from jax.experimental.pallas import tpu as pltpu
from jax.sharding import PartitionSpec as P

BF = jnp.bfloat16
F32 = jnp.float32
I32 = jnp.int32
D = 2560
OWN = 12
PADDED = 16
NT = 8
NE = 64
NTOK = NT * PADDED
ROWS = NE * 8
HID2 = 192
FA = 512
FB = (D - FA) // 4
LA = 1536
LB = (D - LA) // 4
META = 128
SENT_A = 2 * FA + 2 * 2 * LA // 8
SENT_B = FB + 128
GATHERED = ROWS + NE
RA = 1024
RB = 256
SMALL = 24 * 1024 * 1024
LARGE = 60 * 1024 * 1024


def call(kernel, out_shapes, name, flops=0, moved=0, scratch=(), limit=SMALL):
    return pl.pallas_call(
        kernel,
        out_shape=out_shapes,
        scratch_shapes=scratch,
        name=name,
        cost_estimate=pl.CostEstimate(flops=flops, bytes_accessed=moved, transcendentals=0),
        compiler_params=pltpu.CompilerParams(vmem_limit_bytes=limit),
    )


def dot(a, b):
    return jnp.dot(a, b, preferred_element_type=F32)


def dot_t(a, b):
    return lax.dot_general(a, b, (((1,), (1,)), ((), ())), preferred_element_type=F32)


def iota(shape, dim):
    return lax.broadcasted_iota(I32, shape, dim)


def mask(cond):
    return jnp.where(cond, 1.0, 0.0).astype(BF)


def start_kernel(x_ref, dy_ref, ids_ref, gates_ref, msg_ref, all_ref):
    msg_ref[...] = jnp.zeros_like(msg_ref)
    all_ref[...] = jnp.zeros_like(all_ref)
    all_ref[0:OWN, 0:D] = x_ref[...]
    all_ref[0:OWN, D : 2 * D] = dy_ref[...]
    row = iota((6, META), 0)
    lane = iota((6, META), 1)
    place = [jnp.where(lane == row + 6 * i, 1.0, 0.0).astype(BF) for i in range(2)]
    cols = (((0,), (0,)), ((), ()))
    meta = lax.dot_general(
        ids_ref[...].astype(F32).astype(BF), place[0], cols, preferred_element_type=F32
    ) + lax.dot_general(gates_ref[...], place[1], cols, preferred_element_type=F32)
    meta = meta.astype(BF)
    for t in range(NT):
        src = x_ref if t < 4 else dy_ref
        low = FA + FB * (t % 4)
        msg_ref[t, 0:OWN, 0:FB] = src[:, low : low + FB]
        low = LA + LB * (t % 4)
        msg_ref[t, 0:OWN, FB : FB + LB] = src[:, low : low + LB]
        msg_ref[t, 0:OWN, FB + LB : FB + LB + META] = meta


def positions(meta):
    ids = meta.astype(F32).astype(I32)
    lane = iota((NTOK, 128), 1)
    row = iota((NTOK, 128), 0)
    hit = jnp.zeros((NTOK, 128), jnp.bool_)
    for k in range(6):
        hit = hit | ((ids[:, k : k + 1] >> 1) == (lane >> 1))
    member = jnp.where(hit & ((row & 15) < OWN), 1.0, 0.0)
    lower = jnp.where(lane < row, 1.0, 0.0).astype(BF)
    earlier = dot(lower, member.astype(BF))
    return jnp.where(member > 0.5, earlier, -1.0), ids


def one_hots(pos):
    row = iota((ROWS, 128), 0)
    lane = iota((ROWS, 128), 1)
    pick = jnp.where(lane == 2 * (row >> 3), 1.0, 0.0).astype(BF)
    spread = dot_t(pick, pos.astype(BF)).astype(I32)
    sub = row & 7
    main = jnp.where(spread == sub, 1.0, 0.0).astype(BF)
    left = jnp.where(spread == 8 + (sub >> 2), 1.0, 0.0).astype(BF)
    return main, left


def pack_b_kernel(msg_ref, out_ref):
    meta = msg_ref[:, FB + LB : FB + LB + META]
    pos, ids = positions(meta)
    main, left = one_hots(pos)
    out_ref[:, 0:FB] = dot(main, msg_ref[:, 0:FB]).astype(BF)
    row = iota((ROWS, 128), 0)
    sub = row & 7
    pick = mask(iota((ROWS, 128), 1) == 2 * (row >> 3))
    spread = dot_t(pick, pos.astype(BF)).astype(I32)
    tiles = dot(mask(spread == 8 + (sub >> 1)), msg_ref[:, FB : FB + LB])
    tile = jnp.where((sub & 1) == 0, tiles[:, 0:128], tiles[:, 128:256])
    gates = meta.astype(F32)
    lane = iota((NTOK, 128), 1)
    weight = jnp.zeros((NTOK, 128), F32)
    for k in range(6):
        weight = weight + jnp.where(ids[:, k : k + 1] == lane, gates[:, 6 + k : 7 + k], 0.0)
    row16 = iota((16, 128), 0)
    gate_of = jnp.zeros((16, 128), F32)
    for s in range(10):
        col = jnp.sum(jnp.where(pos == float(s), weight, 0.0), axis=0, keepdims=True)
        gate_of = jnp.where(row16 == s, col, gate_of)
    gate_of = jnp.concatenate([gate_of, jnp.zeros((112, 128), F32)], axis=0).astype(BF)
    pick = mask((iota((ROWS, 128), 1) == 2 * (row >> 3) + (sub & 1)) & ((sub >> 1) == 2))
    out_ref[:, FB : FB + 128] = jnp.where(sub < 4, tile, dot_t(pick, gate_of)).astype(BF)


def unpack_b_kernel(in_ref, out_ref, gate_ref):
    out_ref[0:ROWS, :] = in_ref[:, 0:FB]
    row = iota((ROWS, ROWS), 0)
    col = iota((ROWS, ROWS), 1)
    turn = mask(((col & 7) == (row >> 6)) & ((col >> 3) == (row & 63)))
    turned = dot(turn, in_ref[:, FB : FB + 128])
    for r in range(4):
        out_ref[ROWS : ROWS + 64, 128 * r : 128 * (r + 1)] = turned[64 * r : 64 * (r + 1)].astype(BF)
    spread = mask((iota((ROWS, 64), 0) >> 3) == iota((ROWS, 64), 1))
    wide = iota((ROWS, 128), 1)
    sub = iota((ROWS, 128), 0) & 7
    main = jnp.zeros((ROWS, 128), F32)
    rest = jnp.zeros((128, 128), F32)
    lane = iota((128, 128), 1)
    for e in range(2):
        own = turned[64 * (4 + e) : 64 * (5 + e)]
        both = jnp.where(wide == sub, dot(spread, own.astype(BF)), 0.0)
        main = jnp.where(wide == e, jnp.sum(both, axis=1, keepdims=True), main)
        column = jnp.concatenate([own[:, 8:9], own[:, 9:10]], axis=0)
        rest = jnp.where(lane == e, column, rest)
    gate_ref[0:ROWS, :] = main
    gate_ref[ROWS : ROWS + 128, :] = rest


def pack_a_kernel(msg_ref, x_ref, out_ref):
    pos, _ = positions(msg_ref[:, FB + LB : FB + LB + META])
    main, left = one_hots(pos)
    sub4 = iota((ROWS, 128), 0) & 3
    for part in range(2):
        out_ref[:, part * FA : (part + 1) * FA] = dot(main, x_ref[:, part * D : part * D + FA]).astype(BF)
        for q in range(LA // 512):
            low = part * D + 512 * q
            spread = dot(left, x_ref[:, low : low + 512])
            out = spread[:, 0:128]
            for k in range(1, 4):
                out = jnp.where(sub4 == k, spread[:, 128 * k : 128 * (k + 1)], out)
            low = 2 * FA + 128 * (part * (LA // 512) + q)
            out_ref[:, low : low + 128] = out.astype(BF)


def gathered_kernel(b_ref, wg_ref, wu_ref, wd_ref, gate_ref, up_ref, down_ref, x_ref, y_ref):
    wg = wg_ref[...].reshape(HID2, D)
    wu = wu_ref[...].reshape(HID2, D)
    wd = wd_ref[...].reshape(HID2, D)
    gate_pre = up_pre = back_proj = 0.0
    for t in range(4):
        cols = slice(FA + FB * t, FA + FB * (t + 1))
        x0, y0 = GATHERED * t, GATHERED * (t + 4)
        rows = b_ref[x0 : x0 + ROWS, :]
        gate_pre = gate_pre + dot_t(rows, wg[:, cols])
        up_pre = up_pre + dot_t(rows, wu[:, cols])
        back_proj = back_proj + dot_t(b_ref[y0 : y0 + ROWS, :], wd[:, cols])
        for s in range(2):
            x_ref[64 * s : 64 * s + 64, LB * t : LB * (t + 1)] = b_ref[
                x0 + ROWS : x0 + GATHERED, LB * s : LB * (s + 1)
            ]
            y_ref[64 * s : 64 * s + 64, LB * t : LB * (t + 1)] = b_ref[
                y0 + ROWS : y0 + GATHERED, LB * s : LB * (s + 1)
            ]
    gate_ref[0:ROWS, :] = gate_pre
    up_ref[0:ROWS, :] = up_pre
    down_ref[0:ROWS, :] = back_proj
    gate_ref[ROWS : ROWS + 128, :] = dot_t(x_ref[...], wg[:, LA:D])
    up_ref[ROWS : ROWS + 128, :] = dot_t(x_ref[...], wu[:, LA:D])
    down_ref[ROWS : ROWS + 128, :] = dot_t(y_ref[...], wd[:, LA:D])


def perm(inverse):
    row = iota((ROWS, ROWS), 0)
    col = iota((ROWS, ROWS), 1)
    if inverse:
        row, col = col, row
    return jnp.where(((col & 7) == (row >> 6)) & ((col >> 3) == (row & 63)), 1.0, 0.0).astype(BF)


def grads(gate_pre, up_pre, back_proj, gates):
    lane = iota(gate_pre.shape, 1)
    scaled = back_proj * jnp.where(lane < HID2 // 2, gates[0], gates[1])
    sig = 1.0 / (1.0 + jnp.exp(-gate_pre))
    up_grad = (scaled * gate_pre * sig).astype(BF)
    gate_grad = (scaled * up_pre * sig * (1.0 + gate_pre * (1.0 - sig))).astype(BF)
    return gate_grad, up_grad


def sum_kernel(
    a_ref,
    gates_ref,
    gate_ref,
    up_ref,
    down_ref,
    wg_ref,
    wu_ref,
    wd_ref,
    rs_ref,
    main_ref,
    rest_ref,
    left_ref,
):
    wg = wg_ref[...].reshape(HID2, D)
    wu = wu_ref[...].reshape(HID2, D)
    wd = wd_ref[...].reshape(HID2, D)
    turned = dot(perm(False), a_ref[:, 2 * FA : SENT_A]).astype(BF)
    for q in range(2 * LA // 512):
        for s in range(2):
            for k in range(4):
                left_ref[64 * s : 64 * s + 64, 512 * q + 128 * k : 512 * q + 128 * (k + 1)] = turned[
                    64 * (4 * s + k) : 64 * (4 * s + k + 1), 128 * q : 128 * (q + 1)
                ]
    own = slice(0, ROWS)
    gate_grad, up_grad = grads(
        gate_ref[own, :] + dot_t(a_ref[:, 0:FA], wg[:, 0:FA]),
        up_ref[own, :] + dot_t(a_ref[:, 0:FA], wu[:, 0:FA]),
        down_ref[own, :] + dot_t(a_ref[:, FA : 2 * FA], wd[:, 0:FA]),
        (gates_ref[own, 0:1], gates_ref[own, 1:2]),
    )
    own = slice(ROWS, ROWS + 128)
    gate_left, up_left = grads(
        gate_ref[own, :] + dot_t(left_ref[:, 0:LA], wg[:, 0:LA]),
        up_ref[own, :] + dot_t(left_ref[:, 0:LA], wu[:, 0:LA]),
        down_ref[own, :] + dot_t(left_ref[:, LA : 2 * LA], wd[:, 0:LA]),
        (gates_ref[own, 0:1], gates_ref[own, 1:2]),
    )
    main_ref[0], main_ref[1] = gate_grad, up_grad
    rest_ref[0], rest_ref[1] = gate_left, up_left

    def part(low, width):
        cols = slice(low, low + width)
        return (
            dot(gate_grad, wg[:, cols]) + dot(up_grad, wu[:, cols]),
            dot(gate_left, wg[:, cols]) + dot(up_left, wu[:, cols]),
        )

    row = iota((ROWS, 768), 0)
    col = iota((ROWS, 768), 1)
    sub = row & 7
    first = (col < 512) & ((col >> 3) == (row >> 3)) & (((col & 7) >> 1) == sub)
    rest = (col >= 512) & ((col & 63) == (row >> 3))
    slot = (col >> 6) & 3
    rest = rest & (((slot < 2) & (sub == 4 + slot)) | ((slot >= 2) & (sub == 6)))
    place = jnp.where(first | rest, 1.0, 0.0).astype(BF)

    def halves(tile, odd_rows, odd_slice):
        low_half = iota(tile.shape, 1) < 64
        moved = pltpu.roll(tile, 64, 1)
        both = jnp.where(low_half, moved, tile) if odd_slice else jnp.where(low_half, tile, moved)
        return jnp.where(low_half == odd_rows, 0.0, both).astype(BF)

    odd_main = (iota((ROWS, 128), 0) & 1) == 1
    odd_left = iota((128, 128), 0) >= 64
    for c in range(2):
        half_main, half_left = part(2048 + 256 * c, 256)
        for pair in range(2):
            t0 = 4 * c + 2 * pair
            full_main, full_left = part(RA + 128 * t0, 256)
            tile_main = half_main[:, 128 * pair : 128 * (pair + 1)]
            tile_left = half_left[:, 128 * pair : 128 * (pair + 1)]
            for i in range(2):
                stack = jnp.concatenate(
                    [
                        halves(tile_main, odd_main, i == 1),
                        full_left[:, 128 * i : 128 * (i + 1)].astype(BF),
                        halves(tile_left, odd_left, i == 1),
                    ],
                    axis=0,
                )
                rs_ref[t0 + i, :, 0:128] = full_main[:, 128 * i : 128 * (i + 1)].astype(BF)
                rs_ref[t0 + i, :, 128:256] = dot(place, stack).astype(BF)


def direct_kernel(main_ref, rest_ref, wg_ref, wu_ref, out_ref, z_ref):
    wg = wg_ref[...].reshape(HID2, D)
    wu = wu_ref[...].reshape(HID2, D)
    out_ref[:, 0:RA] = (dot(main_ref[0], wg[:, 0:RA]) + dot(main_ref[1], wu[:, 0:RA])).astype(BF)
    part = (dot(rest_ref[0], wg[:, 0:RA]) + dot(rest_ref[1], wu[:, 0:RA])).astype(BF)
    for q in range(RA // 512):
        for s in range(2):
            for k in range(4):
                low = 512 * q + 128 * k
                z_ref[64 * (4 * s + k) : 64 * (4 * s + k + 1), 128 * q : 128 * (q + 1)] = part[
                    64 * s : 64 * s + 64, low : low + 128
                ]
    out_ref[:, RA : RA + RA // 4] = dot(perm(True), z_ref[...]).astype(BF)


def spread_positions(msg_ref):
    pos, _ = positions(msg_ref[:, FB + LB : FB + LB + META])
    row = iota((128, ROWS), 0)
    col = iota((128, ROWS), 1)
    pick = jnp.where(row == 2 * (col >> 3), 1.0, 0.0).astype(BF)
    return dot(pos.astype(BF), pick).astype(I32), col & 7


def combine_a_kernel(msg_ref, a_ref, out_ref):
    spread, sub = spread_positions(msg_ref)
    main = mask(spread == sub)
    total = dot(main, a_ref[:, 0:RA])
    for k in range(4):
        left = mask((spread == 8 + (sub >> 2)) & ((sub & 3) == k))
        rest = dot(left, a_ref[:, RA : RA + RA // 4])
        for q in range(RA // 512):
            low = 512 * q + 128 * k
            out_ref[:, low : low + 128] = (
                total[:, low : low + 128] + rest[:, 128 * q : 128 * (q + 1)]
            ).astype(BF)


def combine_b_kernel(msg_ref, b_ref, a_ref, out_ref):
    spread, sub = spread_positions(msg_ref)
    out_ref[:, 0:RA] = a_ref[...]
    main = mask(spread == sub)
    tile = b_ref[:, 128:256]
    rest = mask(((sub == 4) & (spread == 8)) | ((sub == 5) & (spread == 9)))
    out_ref[:, RA : RA + 128] = (dot(main, b_ref[:, 0:128]) + dot(rest, tile)).astype(BF)
    low = dot(mask(((sub < 4) & (spread == 2 * sub)) | ((sub == 6) & (spread == 8))), tile)
    high = dot(mask(((sub < 4) & (spread == 2 * sub + 1)) | ((sub == 6) & (spread == 9))), tile)
    both = jnp.where(iota((NTOK, 128), 1) < 64, low, high)
    out_ref[:, RA + 128 : RA + 256] = (both + pltpu.roll(both, 64, 1)).astype(BF)


def finish_kernel(in_ref, out_ref):
    total = in_ref[0, :, 0:RA].astype(F32)
    for t in range(1, NT):
        total = total + in_ref[t, :, 0:RA].astype(F32)
    out_ref[:, 0:RA] = total.astype(BF)[0:OWN]
    for t in range(NT):
        low = RA + 128 * t
        out_ref[:, low : low + 128] = in_ref[t, 0:OWN, RA : RA + 128]
    low_half = iota((PADDED, 128), 1) < 64
    for t in range(0, NT, 2):
        low = 2048 + 64 * t
        tile = jnp.where(
            low_half,
            in_ref[t, :, RA + 128 : RA + 256].astype(F32),
            in_ref[t + 1, :, RA + 128 : RA + 256].astype(F32),
        )
        out_ref[:, low : low + 128] = tile.astype(BF)[0:OWN]


def shape(*dims, dtype=BF):
    return jax.ShapeDtypeStruct(dims, dtype)


def per_device(tokens, out_grad, expert_ids, gate_values, gate_weight, up_weight, down_weight):
    weights = (gate_weight, up_weight, down_weight)
    lanes = FB + LB + META
    msg, both = call(start_kernel, (shape(NT, PADDED, lanes), shape(PADDED, 2 * D)), "start", limit=LARGE)(
        tokens, out_grad, expert_ids.T, gate_values.T
    )
    both_all = lax.all_gather(both, "tensor", axis=0, tiled=True)
    msg = lax.all_to_all(msg, "tensor", 0, 0, tiled=True).reshape(NTOK, lanes)
    send_b = call(pack_b_kernel, shape(ROWS, SENT_B), "pack_b", flops=2 * ROWS * 128 * 1280)(msg)
    recv_b = lax.all_to_all(send_b.reshape(NE, 8, SENT_B), "expert", 0, 0, tiled=True)
    own_b, gates = call(
        unpack_b_kernel,
        (shape(GATHERED, FB), shape(ROWS + 128, 128, dtype=F32)),
        "unpack_b",
        flops=2 * ROWS * ROWS * 128,
    )(recv_b.reshape(ROWS, SENT_B))
    all_b = lax.all_gather(own_b, "tensor", axis=0, tiled=True)
    send_a = call(pack_a_kernel, shape(ROWS, SENT_A), "pack_a", flops=2 * ROWS * 128 * 4096)(msg, both_all)
    recv_a = lax.all_to_all(send_a.reshape(NE, 8, SENT_A), "expert", 0, 0, tiled=True)
    pre = call(
        gathered_kernel,
        (shape(ROWS + 128, HID2, dtype=F32),) * 3,
        "gathered",
        flops=6 * ROWS * 2048 * HID2,
        moved=8_000_000,
        scratch=[pltpu.VMEM((128, D - LA), BF), pltpu.VMEM((128, D - LA), BF)],
        limit=LARGE,
    )(all_b, *weights)
    to_sum, main, rest = call(
        sum_kernel,
        (shape(NT, ROWS, RB), shape(2, ROWS, HID2), shape(2, 128, HID2)),
        "sum",
        flops=6 * 640 * D * HID2,
        moved=10_000_000,
        scratch=[pltpu.VMEM((128, 2 * LA), BF)],
        limit=LARGE,
    )(recv_a.reshape(ROWS, SENT_A), gates, *pre, *weights)
    summed = lax.psum_scatter(to_sum, "tensor", scatter_dimension=0, tiled=False)
    to_send = call(
        direct_kernel,
        shape(ROWS, RA + RA // 4),
        "direct",
        flops=4 * 640 * RA * HID2,
        moved=4_000_000,
        scratch=[pltpu.VMEM((ROWS, RA // 4), BF)],
        limit=LARGE,
    )(main, rest, gate_weight, up_weight)
    back_a = lax.all_to_all(to_send.reshape(NE, 8, RA + RA // 4), "expert", 0, 0, tiled=True)
    back_b = lax.all_to_all(summed.reshape(NE, 8, RB), "expert", 0, 0, tiled=True)
    part_a = call(combine_a_kernel, shape(NTOK, RA), "combine_a", flops=2 * ROWS * 128 * 2048)(
        msg, back_a.reshape(ROWS, RA + RA // 4)
    )
    last = call(combine_b_kernel, shape(NTOK, RA + RB), "combine_b", flops=2 * ROWS * 128 * 512)(
        msg, back_b.reshape(ROWS, RB), part_a
    )
    last = lax.all_to_all(last.reshape(NT, PADDED, RA + RB), "tensor", 0, 0, tiled=True)
    return call(finish_kernel, shape(OWN, D), "finish")(last)


def solution(mesh):
    return jax.shard_map(
        per_device,
        mesh=mesh,
        in_specs=(
            P(("expert", "tensor"), None),
            P(("expert", "tensor"), None),
            P(("expert", "tensor"), None),
            P(("expert", "tensor"), None),
            P("expert", "tensor", None),
            P("expert", "tensor", None),
            P("expert", "tensor", None),
        ),
        out_specs=P(("expert", "tensor"), None),
        check_vma=False,
    )
```

time: 593 us -> 231 us (0.39)
  blocking collectives: 365 us -> 114 us
  waiting for transfers between devices: 106 us -> 57.9 us
  local copies, waits for them, and re-layouts: 47.9 us -> 3.28 us
  Pallas kernels: 0 us -> 29.6 us
  matrix products: 23.3 us -> 0 us
  starting transfers between devices: 34.1 us -> 12.5 us
  between operations: 0.89 us -> 13.2 us
  other arithmetic: 10.1 us -> 0 us
    all_to_all x2 -> x4, blocking collectives: 264 us -> 114 us  [the longest x1 44 us: per_device(): lax.all_to_all(to_send.reshape(NE, 8, RA + RA // 4), 'expert', 0, 0, tile...]
    all_to_all x2, waiting for transfers between devices: 106 us -> 12.3 us  [the longest x1 12.3 us: per_device(): lax.all_to_all(summed.reshape(NE, 8, RB), 'expert', 0, 0, tiled=True)]
    all_gather x4 -> x0, blocking collectives: 82.2 us -> none  [the longest x1 25.5 us: per_device(): group_ids = lax.all_gather(expert_ids, 'tensor', axis=0, tiled=True)]
    all_gather x0 -> x2, waiting for transfers between devices: none -> 45.6 us  [the longest x1 45.6 us: per_device(): all_b = lax.all_gather(own_b, 'tensor', axis=0, tiled=True)]
    pallas_call x0 -> x10, Pallas kernels: none -> 29.6 us  [the longest x1 9.06 us: per_device(): call(sum_kernel, (shape(NT, ROWS, RB), shape(2, ROWS, HID2), shape(2, 128...]
    dot_general x5 -> x0, matrix products: 23.3 us -> none  [the longest x1 7.34 us: expert_terms(): jnp.einsum('erh,ehf->rf', gate_grad, gate_weight, preferred_element_type=...]
    gather x4 -> x0, local copies, waits for them, and re-layouts: 22.5 us -> none  [pick_rows(): return jnp.take(padded, source, axis=0)]
    reshape x3 -> x0, local copies, waits for them, and re-layouts: 20.9 us -> none  [the longest x1 7.02 us: per_device(): recv_x.reshape(flat_rows, feature_width)]
  transfers between devices with their start and end apart: 4 -> 5, of which waited for: 1 -> 2; matrix products, arithmetic and copies ran while one was open for 8% -> 0% of each run, Pallas kernels for 0% -> 7%
where the time goes in v2:
time: 231 us; the launch traced here: 230 us
  blocking collectives  114 us (49%)
  waiting for transfers between devices  57.9 us (25%)
  Pallas kernels  29.6 us (13%)
  between operations  13.2 us (6%)
  starting transfers between devices  12.5 us (5%)
  local copies, waits for them, and re-layouts  3.28 us (1%)
    all_gather x1, waiting for transfers between devices, per_device(): all_b = lax.all_gather(own_b, 'tensor', axis=0, tiled=True)  45.6 us
    all_to_all x1, blocking collectives, per_device(): lax.all_to_all(to_send.reshape(NE, 8, RA + RA // 4), 'expert', 0, 0, tile...  44 us
    all_to_all x1, blocking collectives, per_device(): lax.all_to_all(send_b.reshape(NE, 8, SENT_B), 'expert', 0, 0, tiled=True)  32.7 us
    all_to_all x1, blocking collectives, per_device(): msg = lax.all_to_all(msg, 'tensor', 0, 0, tiled=True).reshape(NTOK, lanes)  20.6 us
    all_to_all x1, blocking collectives, per_device(): lax.all_to_all(last.reshape(NT, PADDED, RA + RB), 'tensor', 0, 0, tiled=T...  16.5 us
    all_to_all x1, waiting for transfers between devices, per_device(): lax.all_to_all(summed.reshape(NE, 8, RB), 'expert', 0, 0, tiled=True)  12.3 us
    pallas_call x1, Pallas kernels, per_device(): call(sum_kernel, (shape(NT, ROWS, RB), shape(2, ROWS, HID2), shape(2, 128...  9.06 us
    pallas_call x1, Pallas kernels, per_device(): call(gathered_kernel, (shape(ROWS + 128, HID2, dtype=F32),) * 3, 'gathere...  6.39 us
  transfers between devices with their start and end apart: 5, of which 2 were waited for; matrix products, arithmetic and copies ran while one was open for 0% of the time, Pallas kernels for 7%

profile of v2, /device:TPU:1, one launch (start us, length us, event | category | flops | bytes accessed | tf_op | source)
XLA Modules:
  0.0 230.2 jit_solution(8943715095042533231)
XLA Ops:
  6.5 1.8 start.1
  8.4 0.0 all-gather.5.cloned.1.call-start
  8.4 20.6 %all_to_all.30 = bf16[8,16,896]{2,1,0:T(8,128)(2,1)S(1)} all-to-all(bf16[8,16,896]{2,1,0:T(8,128)(2,1)} %get-tuple-element.15), channel_id=1, replica_groups=mesh['tensor'=8,'expert'=64] {'tensor'}, dimensions={0} | all-to-all | bytes 458752 | tf_op jit(solution)/shard_map/all_to_all | solution.py:381
  29.0 0.9 pack_b.1
  30.0 32.7 %all_to_all.31 = bf16[64,8,640]{2,1,0:T(8,128)(2,1)S(1)} all-to-all(bf16[64,8,640]{2,1,0:T(8,128)(2,1)S(1)} %bitcast.18), channel_id=1, replica_groups=mesh['tensor'=8,'expert'=64] {'expert'}, dimensions={0} | all-to-all | bytes 1310720 | tf_op jit(solution)/shard_map/all_to_all | solution.py:383
  62.6 1.5 unpack_b.1
  64.1 0.7 copy-done.1
  64.9 0.0 all-gather.3.cloned.1.call-done.x_ref
  64.9 1.3 copy-done
  66.2 3.1 %pack_a.1 = bf16[512,1792]{1,0:T(8,128)(2,1)} custom-call(bf16[128,896]{1,0:T(8,128)(2,1)S(1)} %bitcast.13, bf16[128,5120]{1,0:T(8,128)(2,1)S(1)} %copy-done), custom_call_target="tpu_custom_call" | custom-call | flops 536870912 | tf_op jit(solution)/shard_map/pack_a/pallas_call | solution.py:391
  69.3 5.9 %all-to-all-start.1 = ((bf16[64,8,1792]{2,1,0:T(8,128)(2,1)}), bf16[64,8,1792]{2,1,0:T(8,128)(2,1)S(1)}, u32[]{:S(2)}, u32[]{:S(2)}) async-start(bf16[64,8,1792]{2,1,0:T(8,128)(2,1)} %bitcast.3), calls=%async_computation.1 | async-start | bytes 3670016 | tf_op jit(solution)/shard_map/all_to_all | solution.py:392
  75.2 0.2 reduce-scatter.2.cloned.1.call-start
  75.4 45.6 %all-gather.5.cloned.1.call-done.b_ref = bf16[4608,512]{1,0:T(8,128)(2,1)} async-done(((bf16[576,512]{1,0:T(8,128)(2,1)}), bf16[4608,512]{1,0:T(8,128)(2,1)}) %all-gather.5.cloned.1.call-update) | async-done | bytes 4718608 | tf_op jit(solution)/shard_map/all_gather | solution.py:390
  121.0 6.4 %gathered.1 = (f32[640,192]{1,0:T(8,128)}, f32[640,192]{1,0:T(8,128)}, f32[640,192]{1,0:T(8,128)}) custom-call(bf16[4608,512]{1,0:T(8,128)(2,1)} %all-gather.5.cloned.1.call-done.b_ref, bf16[2,96,2560]{2,1,0:T(8,128)(2,1)} %wg_ref.5, bf16[2,96,2560]{2,1,0:T(8,128)(2,1)} %wu_ref.5, bf16[2,96,2560]{2,1,0:T(8,128)(2,1)} %wd_ref.3), custom_call_target="tpu_custom_call" | custom-call | flops 1207959552 | bytes 8000000 | tf_op jit(solution)/shard_map/gathered/pallas_call | solution.py:393
  127.4 1.2 copy-done.2
  128.6 9.1 %sum.1 = (bf16[8,512,256]{2,1,0:T(8,128)(2,1)}, bf16[2,512,192]{2,1,0:T(8,128)(2,1)}, bf16[2,128,192]{2,1,0:T(8,128)(2,1)}) custom-call(bf16[512,1792]{1,0:T(8,128)(2,1)} %bitcast.21, f32[640,128]{1,0:T(8,128)} %copy-done.1, f32[640,192]{1,0:T(8,128)} %get-tuple-element.19.gate_ref, f32[640,192]{1,0:T(8,128)} %get-tuple-element.20.up_ref, ...), custom_call_target="tpu_custom_call" | custom-call | flops 1887436800 | bytes 10000000 | tf_op jit(solution)/shard_map/sum/pallas_call | solution.py:402
  137.7 4.2 %direct.1 = bf16[512,1280]{1,0:T(8,128)(2,1)} custom-call(bf16[2,512,192]{2,1,0:T(8,128)(2,1)} %get-tuple-element.23.main_ref, bf16[2,128,192]{2,1,0:T(8,128)(2,1)} %get-tuple-element.24.rest_ref, bf16[2,96,2560]{2,1,0:T(8,128)(2,1)} %wg_ref.5, bf16[2,96,2560]{2,1,0:T(8,128)(2,1)} %wu_ref.5), custom_call_target="tpu_custom_call" | custom-call | flops 503316480 | bytes 4000000 | tf_op jit(solution)/shard_map/direct/pallas_call | solution.py:412
  141.9 44.0 %all_to_all.32 = bf16[64,8,1280]{2,1,0:T(8,128)(2,1)S(1)} all-to-all(bf16[64,8,1280]{2,1,0:T(8,128)(2,1)} %bitcast.22), channel_id=1, replica_groups=mesh['tensor'=8,'expert'=64] {'expert'}, dimensions={0} | all-to-all | bytes 2621440 | tf_op jit(solution)/shard_map/all_to_all | solution.py:421
  185.9 6.3 %all-to-all-start.3 = ((bf16[64,8,256]{2,1,0:T(8,128)(2,1)}), bf16[64,8,256]{2,1,0:T(8,128)(2,1)S(1)}, u32[]{:S(2)}, u32[]{:S(2)}) async-start(bf16[64,8,256]{2,1,0:T(8,128)(2,1)} %bitcast.23), calls=%async_computation.4 | async-start | bytes 524288 | tf_op jit(solution)/shard_map/all_to_all | solution.py:422
  192.2 0.9 combine_a.1.a_ref
  193.1 12.3 %all-to-all-done.3 = bf16[64,8,256]{2,1,0:T(8,128)(2,1)S(1)} async-done(((bf16[64,8,256]{2,1,0:T(8,128)(2,1)}), bf16[64,8,256]{2,1,0:T(8,128)(2,1)S(1)}, u32[]{:S(2)}, u32[]{:S(2)}) %all-to-all-start.3) | async-done | bytes 262176 | tf_op jit(solution)/shard_map/all_to_all | solution.py:422
  205.4 1.1 combine_b.1
  206.5 16.5 %all_to_all.33.in_ref = bf16[8,16,1280]{2,1,0:T(8,128)(2,1)S(1)} all-to-all(bf16[8,16,1280]{2,1,0:T(8,128)(2,1)S(1)} %bitcast.19), channel_id=1, replica_groups=mesh['tensor'=8,'expert'=64] {'tensor'}, dimensions={0} | all-to-all | bytes 655360 | tf_op jit(solution)/shard_map/all_to_all | solution.py:429
  223.0 0.7 finish.1
  (9 shorter events, 0.1 us)
Async XLA Ops:
  6.5 58.4 %all-gather.3.cloned.1.call-start = ((), (), s32[]{:S(2)}) async-start(), calls=%async_computation.7 | async-start | bytes 1474560 | tf_op jit(solution)/shard_map/all_gather | solution.py:380
  8.4 112.7 %all-gather.5.cloned.1.call-start = ((), (), s32[]{:S(2)}) async-start(), calls=%async_computation.8 | async-start | bytes 5308416 | tf_op jit(solution)/shard_map/all_gather | solution.py:390
  64.1 0.8 copy-start.1
  64.9 1.3 copy-start
  69.3 58.1 %all-to-all-start.1 = ((bf16[64,8,1792]{2,1,0:T(8,128)(2,1)}), bf16[64,8,1792]{2,1,0:T(8,128)(2,1)S(1)}, u32[]{:S(2)}, u32[]{:S(2)}) async-start(bf16[64,8,1792]{2,1,0:T(8,128)(2,1)} %bitcast.3), calls=%async_computation.1 | async-start | bytes 3670016 | tf_op jit(solution)/shard_map/all_to_all | solution.py:392
  75.2 110.7 %reduce-scatter.2.cloned.1.call-start = ((), (), s32[]{:S(2)}) async-start(), calls=%async_computation.9 | async-start | bytes 2359296 | tf_op jit(solution)/shard_map/reduce_scatter | solution.py:411
  127.4 1.2 copy-start.2
  185.9 19.5 %all-to-all-start.3 = ((bf16[64,8,256]{2,1,0:T(8,128)(2,1)}), bf16[64,8,256]{2,1,0:T(8,128)(2,1)S(1)}, u32[]{:S(2)}, u32[]{:S(2)}) async-start(bf16[64,8,256]{2,1,0:T(8,128)(2,1)} %bitcast.23), calls=%async_computation.4 | async-start | bytes 524288 | tf_op jit(solution)/shard_map/all_to_all | solution.py:422
Sparse Core Ops, SparseCore 0:
  9.4 43.6 all-gather.2
  65.0 55.9 all-gather.4
  137.8 39.7 reduce-scatter.1

commit v3 on v2

--- a/solution.py
+++ b/solution.py
@@ -30,10 +30,20 @@
 LARGE = 60 * 1024 * 1024
 
 
-def call(kernel, out_shapes, name, flops=0, moved=0, scratch=(), limit=SMALL):
+HBM = pl.BlockSpec(memory_space=pltpu.HBM)
+VMEM = pl.BlockSpec(memory_space=pltpu.VMEM)
+
+
+def call(kernel, out_shapes, name, flops=0, moved=0, scratch=(), limit=SMALL, ins=None, outs=None):
+    specs = {}
+    if ins is not None:
+        specs["in_specs"] = ins
+    if outs is not None:
+        specs["out_specs"] = outs
     return pl.pallas_call(
         kernel,
         out_shape=out_shapes,
+        **specs,
         scratch_shapes=scratch,
         name=name,
         cost_estimate=pl.CostEstimate(flops=flops, bytes_accessed=moved, transcendentals=0),
@@ -129,12 +139,11 @@
     out_ref[:, FB : FB + 128] = jnp.where(sub < 4, tile, dot_t(pick, gate_of)).astype(BF)
 
 
-def unpack_b_kernel(in_ref, out_ref, gate_ref):
+def unpack_b_kernel(in_ref, out_ref, gate_out, gate_ref, sem):
     out_ref[0:ROWS, :] = in_ref[:, 0:FB]
-    row = iota((ROWS, ROWS), 0)
-    col = iota((ROWS, ROWS), 1)
-    turn = mask(((col & 7) == (row >> 6)) & ((col >> 3) == (row & 63)))
-    turned = dot(turn, in_ref[:, FB : FB + 128])
+    turn = perm(False)
+    turned = [dot(turn, in_ref[256 * h : 256 * (h + 1), FB : FB + 128]) for h in range(2)]
+    turned = jnp.concatenate([turned[h][32 * r : 32 * (r + 1)] for r in range(6) for h in range(2)], axis=0)
     for r in range(4):
         out_ref[ROWS : ROWS + 64, 128 * r : 128 * (r + 1)] = turned[64 * r : 64 * (r + 1)].astype(BF)
     spread = mask((iota((ROWS, 64), 0) >> 3) == iota((ROWS, 64), 1))
@@ -151,12 +160,18 @@
         rest = jnp.where(lane == e, column, rest)
     gate_ref[0:ROWS, :] = main
     gate_ref[ROWS : ROWS + 128, :] = rest
-
-
-def pack_a_kernel(msg_ref, x_ref, out_ref):
+    copy = pltpu.make_async_copy(gate_ref, gate_out, sem)
+    copy.start()
+    copy.wait()
+
+
+def pack_a_kernel(msg_ref, x_in, out_ref, x_ref, sem):
+    copy = pltpu.make_async_copy(x_in, x_ref, sem)
+    copy.start()
     pos, _ = positions(msg_ref[:, FB + LB : FB + LB + META])
     main, left = one_hots(pos)
     sub4 = iota((ROWS, 128), 0) & 3
+    copy.wait()
     for part in range(2):
         out_ref[:, part * FA : (part + 1) * FA] = dot(main, x_ref[:, part * D : part * D + FA]).astype(BF)
         for q in range(LA // 512):
@@ -169,39 +184,12 @@
             out_ref[:, low : low + 128] = out.astype(BF)
 
 
-def gathered_kernel(b_ref, wg_ref, wu_ref, wd_ref, gate_ref, up_ref, down_ref, x_ref, y_ref):
-    wg = wg_ref[...].reshape(HID2, D)
-    wu = wu_ref[...].reshape(HID2, D)
-    wd = wd_ref[...].reshape(HID2, D)
-    gate_pre = up_pre = back_proj = 0.0
-    for t in range(4):
-        cols = slice(FA + FB * t, FA + FB * (t + 1))
-        x0, y0 = GATHERED * t, GATHERED * (t + 4)
-        rows = b_ref[x0 : x0 + ROWS, :]
-        gate_pre = gate_pre + dot_t(rows, wg[:, cols])
-        up_pre = up_pre + dot_t(rows, wu[:, cols])
-        back_proj = back_proj + dot_t(b_ref[y0 : y0 + ROWS, :], wd[:, cols])
-        for s in range(2):
-            x_ref[64 * s : 64 * s + 64, LB * t : LB * (t + 1)] = b_ref[
-                x0 + ROWS : x0 + GATHERED, LB * s : LB * (s + 1)
-            ]
-            y_ref[64 * s : 64 * s + 64, LB * t : LB * (t + 1)] = b_ref[
-                y0 + ROWS : y0 + GATHERED, LB * s : LB * (s + 1)
-            ]
-    gate_ref[0:ROWS, :] = gate_pre
-    up_ref[0:ROWS, :] = up_pre
-    down_ref[0:ROWS, :] = back_proj
-    gate_ref[ROWS : ROWS + 128, :] = dot_t(x_ref[...], wg[:, LA:D])
-    up_ref[ROWS : ROWS + 128, :] = dot_t(x_ref[...], wu[:, LA:D])
-    down_ref[ROWS : ROWS + 128, :] = dot_t(y_ref[...], wd[:, LA:D])
-
-
 def perm(inverse):
-    row = iota((ROWS, ROWS), 0)
-    col = iota((ROWS, ROWS), 1)
+    row = iota((256, 256), 0)
+    col = iota((256, 256), 1)
     if inverse:
         row, col = col, row
-    return jnp.where(((col & 7) == (row >> 6)) & ((col >> 3) == (row & 63)), 1.0, 0.0).astype(BF)
+    return mask(((col & 7) == (row >> 5)) & ((col >> 3) == (row & 31)))
 
 
 def grads(gate_pre, up_pre, back_proj, gates):
@@ -213,46 +201,79 @@
     return gate_grad, up_grad
 
 
-def sum_kernel(
+def experts_kernel(
+    a_in,
+    b_in,
+    gates_in,
+    wg_in,
+    wu_in,
+    wd_in,
+    rs_out,
+    send_ref,
     a_ref,
+    b_ref,
     gates_ref,
-    gate_ref,
-    up_ref,
-    down_ref,
     wg_ref,
     wu_ref,
     wd_ref,
+    left_ref,
+    z_ref,
     rs_ref,
-    main_ref,
-    rest_ref,
-    left_ref,
+    sems,
+    out_sems,
 ):
+    pairs = [(wg_in, wg_ref), (wu_in, wu_ref), (wd_in, wd_ref), (a_in, a_ref), (gates_in, gates_ref)]
+    for t in (0, 4, 1, 5, 2, 6, 3, 7):
+        rows = pl.ds(GATHERED * t, GATHERED)
+        pairs.append((b_in.at[rows], b_ref.at[rows]))
+    copies = [pltpu.make_async_copy(src, dst, sems.at[i]) for i, (src, dst) in enumerate(pairs)]
+    for copy in copies:
+        copy.start()
+    turn = perm(False)
+    turn_back = perm(True)
+    for copy in copies[:4]:
+        copy.wait()
     wg = wg_ref[...].reshape(HID2, D)
     wu = wu_ref[...].reshape(HID2, D)
     wd = wd_ref[...].reshape(HID2, D)
-    turned = dot(perm(False), a_ref[:, 2 * FA : SENT_A]).astype(BF)
-    for q in range(2 * LA // 512):
-        for s in range(2):
-            for k in range(4):
-                left_ref[64 * s : 64 * s + 64, 512 * q + 128 * k : 512 * q + 128 * (k + 1)] = turned[
-                    64 * (4 * s + k) : 64 * (4 * s + k + 1), 128 * q : 128 * (q + 1)
+    for h in range(2):
+        turned = dot(turn, a_ref[256 * h : 256 * (h + 1), 2 * FA : SENT_A]).astype(BF)
+        for q in range(2 * LA // 512):
+            base = (q // (LA // 512)) * D + 512 * (q % (LA // 512))
+            for s in range(2):
+                for k in range(4):
+                    low = 64 * s + 32 * h
+                    left_ref[low : low + 32, base + 128 * k : base + 128 * (k + 1)] = turned[
+                        32 * (4 * s + k) : 32 * (4 * s + k + 1), 128 * q : 128 * (q + 1)
+                    ]
+    gate_pre = dot_t(a_ref[:, 0:FA], wg[:, 0:FA])
+    up_pre = dot_t(a_ref[:, 0:FA], wu[:, 0:FA])
+    back_proj = dot_t(a_ref[:, FA : 2 * FA], wd[:, 0:FA])
+    copies[4].wait()
+    for t in range(4):
+        copies[5 + 2 * t].wait()
+        copies[6 + 2 * t].wait()
+        cols = slice(FA + FB * t, FA + FB * (t + 1))
+        x0, y0 = GATHERED * t, GATHERED * (t + 4)
+        rows = b_ref[x0 : x0 + ROWS, :]
+        gate_pre = gate_pre + dot_t(rows, wg[:, cols])
+        up_pre = up_pre + dot_t(rows, wu[:, cols])
+        back_proj = back_proj + dot_t(b_ref[y0 : y0 + ROWS, :], wd[:, cols])
+        for base, start in ((0, x0), (D, y0)):
+            low = base + LA + LB * t
+            for s in range(2):
+                left_ref[64 * s : 64 * s + 64, low : low + LB] = b_ref[
+                    start + ROWS : start + GATHERED, LB * s : LB * (s + 1)
                 ]
-    own = slice(0, ROWS)
+    gate_left, up_left = grads(
+        dot_t(left_ref[:, 0:D], wg),
+        dot_t(left_ref[:, 0:D], wu),
+        dot_t(left_ref[:, D : 2 * D], wd),
+        (gates_ref[ROWS : ROWS + 128, 0:1], gates_ref[ROWS : ROWS + 128, 1:2]),
+    )
     gate_grad, up_grad = grads(
-        gate_ref[own, :] + dot_t(a_ref[:, 0:FA], wg[:, 0:FA]),
-        up_ref[own, :] + dot_t(a_ref[:, 0:FA], wu[:, 0:FA]),
-        down_ref[own, :] + dot_t(a_ref[:, FA : 2 * FA], wd[:, 0:FA]),
-        (gates_ref[own, 0:1], gates_ref[own, 1:2]),
-    )
-    own = slice(ROWS, ROWS + 128)
-    gate_left, up_left = grads(
-        gate_ref[own, :] + dot_t(left_ref[:, 0:LA], wg[:, 0:LA]),
-        up_ref[own, :] + dot_t(left_ref[:, 0:LA], wu[:, 0:LA]),
-        down_ref[own, :] + dot_t(left_ref[:, LA : 2 * LA], wd[:, 0:LA]),
-        (gates_ref[own, 0:1], gates_ref[own, 1:2]),
-    )
-    main_ref[0], main_ref[1] = gate_grad, up_grad
-    rest_ref[0], rest_ref[1] = gate_left, up_left
+        gate_pre, up_pre, back_proj, (gates_ref[0:ROWS, 0:1], gates_ref[0:ROWS, 1:2])
+    )
 
     def part(low, width):
         cols = slice(low, low + width)
@@ -261,14 +282,15 @@
             dot(gate_left, wg[:, cols]) + dot(up_left, wu[:, cols]),
         )
 
-    row = iota((ROWS, 768), 0)
-    col = iota((ROWS, 768), 1)
+    row = iota((256, 256), 0)
+    col = iota((256, 256), 1)
+    place_main = mask(((col >> 3) == (row >> 3)) & (((col & 7) >> 1) == (row & 7)))
+    row = iota((ROWS, 256), 0)
+    col = iota((ROWS, 256), 1)
     sub = row & 7
-    first = (col < 512) & ((col >> 3) == (row >> 3)) & (((col & 7) >> 1) == sub)
-    rest = (col >= 512) & ((col & 63) == (row >> 3))
-    slot = (col >> 6) & 3
-    rest = rest & (((slot < 2) & (sub == 4 + slot)) | ((slot >= 2) & (sub == 6)))
-    place = jnp.where(first | rest, 1.0, 0.0).astype(BF)
+    slot = col >> 6
+    fits = ((slot < 2) & (sub == 4 + slot)) | ((slot >= 2) & (sub == 6))
+    place_left = mask(((col & 63) == (row >> 3)) & fits)
 
     def halves(tile, odd_rows, odd_slice):
         low_half = iota(tile.shape, 1) < 64
@@ -278,6 +300,7 @@
 
     odd_main = (iota((ROWS, 128), 0) & 1) == 1
     odd_left = iota((128, 128), 0) >= 64
+    outs = []
     for c in range(2):
         half_main, half_left = part(2048 + 256 * c, 256)
         for pair in range(2):
@@ -285,32 +308,40 @@
             full_main, full_left = part(RA + 128 * t0, 256)
             tile_main = half_main[:, 128 * pair : 128 * (pair + 1)]
             tile_left = half_left[:, 128 * pair : 128 * (pair + 1)]
+            mains = jnp.concatenate([halves(tile_main, odd_main, i == 1) for i in range(2)], axis=1)
+            lefts = jnp.concatenate(
+                [
+                    full_left.astype(BF),
+                    jnp.concatenate([halves(tile_left, odd_left, i == 1) for i in range(2)], axis=1),
+                ],
+                axis=0,
+            )
+            placed = dot(place_left, lefts)
+            for h in range(2):
+                rows = slice(256 * h, 256 * (h + 1))
+                both = (placed[rows] + dot(place_main, mains[rows])).astype(BF)
+                for i in range(2):
+                    rs_ref[t0 + i, rows, 128:256] = both[:, 128 * i : 128 * (i + 1)]
             for i in range(2):
-                stack = jnp.concatenate(
-                    [
-                        halves(tile_main, odd_main, i == 1),
-                        full_left[:, 128 * i : 128 * (i + 1)].astype(BF),
-                        halves(tile_left, odd_left, i == 1),
-                    ],
-                    axis=0,
-                )
                 rs_ref[t0 + i, :, 0:128] = full_main[:, 128 * i : 128 * (i + 1)].astype(BF)
-                rs_ref[t0 + i, :, 128:256] = dot(place, stack).astype(BF)
-
-
-def direct_kernel(main_ref, rest_ref, wg_ref, wu_ref, out_ref, z_ref):
-    wg = wg_ref[...].reshape(HID2, D)
-    wu = wu_ref[...].reshape(HID2, D)
-    out_ref[:, 0:RA] = (dot(main_ref[0], wg[:, 0:RA]) + dot(main_ref[1], wu[:, 0:RA])).astype(BF)
-    part = (dot(rest_ref[0], wg[:, 0:RA]) + dot(rest_ref[1], wu[:, 0:RA])).astype(BF)
+                outs.append(pltpu.make_async_copy(rs_ref.at[t0 + i], rs_out.at[t0 + i], out_sems.at[t0 + i]))
+                outs[-1].start()
     for q in range(RA // 512):
-        for s in range(2):
-            for k in range(4):
-                low = 512 * q + 128 * k
-                z_ref[64 * (4 * s + k) : 64 * (4 * s + k + 1), 128 * q : 128 * (q + 1)] = part[
-                    64 * s : 64 * s + 64, low : low + 128
-                ]
-    out_ref[:, RA : RA + RA // 4] = dot(perm(True), z_ref[...]).astype(BF)
+        sums, rest = part(512 * q, 512)
+        send_ref[:, 512 * q : 512 * (q + 1)] = sums.astype(BF)
+        rest = rest.astype(BF)
+        for h in range(2):
+            for s in range(2):
+                for k in range(4):
+                    low = 32 * (4 * s + k)
+                    z_ref[256 * h + low : 256 * h + low + 32, 128 * q : 128 * (q + 1)] = rest[
+                        64 * s + 32 * h : 64 * s + 32 * h + 32, 128 * k : 128 * (k + 1)
+                    ]
+    for h in range(2):
+        rows = slice(256 * h, 256 * (h + 1))
+        send_ref[rows, RA : RA + RA // 4] = dot(turn_back, z_ref[rows, :]).astype(BF)
+    for copy in outs:
+        copy.wait()
 
 
 def spread_positions(msg_ref):
@@ -386,38 +417,43 @@
         (shape(GATHERED, FB), shape(ROWS + 128, 128, dtype=F32)),
         "unpack_b",
         flops=2 * ROWS * ROWS * 128,
+        scratch=[pltpu.VMEM((ROWS + 128, 128), F32), pltpu.SemaphoreType.DMA],
+        outs=(VMEM, HBM),
     )(recv_b.reshape(ROWS, SENT_B))
     all_b = lax.all_gather(own_b, "tensor", axis=0, tiled=True)
-    send_a = call(pack_a_kernel, shape(ROWS, SENT_A), "pack_a", flops=2 * ROWS * 128 * 4096)(msg, both_all)
+    send_a = call(
+        pack_a_kernel,
+        shape(ROWS, SENT_A),
+        "pack_a",
+        flops=2 * ROWS * 128 * 4096,
+        scratch=[pltpu.VMEM((NTOK, 2 * D), BF), pltpu.SemaphoreType.DMA],
+        ins=[VMEM, HBM],
+    )(msg, both_all)
     recv_a = lax.all_to_all(send_a.reshape(NE, 8, SENT_A), "expert", 0, 0, tiled=True)
-    pre = call(
-        gathered_kernel,
-        (shape(ROWS + 128, HID2, dtype=F32),) * 3,
-        "gathered",
-        flops=6 * ROWS * 2048 * HID2,
-        moved=8_000_000,
-        scratch=[pltpu.VMEM((128, D - LA), BF), pltpu.VMEM((128, D - LA), BF)],
+    to_sum, to_send = call(
+        experts_kernel,
+        (shape(NT, ROWS, RB), shape(ROWS, RA + RA // 4)),
+        "experts",
+        flops=10 * 640 * D * HID2,
+        moved=13_000_000,
+        scratch=[
+            pltpu.VMEM((ROWS, SENT_A), BF),
+            pltpu.VMEM((NT * GATHERED, FB), BF),
+            pltpu.VMEM((ROWS + 128, 128), F32),
+            pltpu.VMEM((2, HID2 // 2, D), BF),
+            pltpu.VMEM((2, HID2 // 2, D), BF),
+            pltpu.VMEM((2, HID2 // 2, D), BF),
+            pltpu.VMEM((128, 2 * D), BF),
+            pltpu.VMEM((ROWS, RA // 4), BF),
+            pltpu.VMEM((NT, ROWS, RB), BF),
+            pltpu.SemaphoreType.DMA((5 + NT,)),
+            pltpu.SemaphoreType.DMA((NT,)),
+        ],
         limit=LARGE,
-    )(all_b, *weights)
-    to_sum, main, rest = call(
-        sum_kernel,
-        (shape(NT, ROWS, RB), shape(2, ROWS, HID2), shape(2, 128, HID2)),
-        "sum",
-        flops=6 * 640 * D * HID2,
-        moved=10_000_000,
-        scratch=[pltpu.VMEM((128, 2 * LA), BF)],
-        limit=LARGE,
-    )(recv_a.reshape(ROWS, SENT_A), gates, *pre, *weights)
+        ins=[HBM] * 6,
+        outs=(HBM, VMEM),
+    )(recv_a.reshape(ROWS, SENT_A), all_b, gates, *weights)
     summed = lax.psum_scatter(to_sum, "tensor", scatter_dimension=0, tiled=False)
-    to_send = call(
-        direct_kernel,
-        shape(ROWS, RA + RA // 4),
-        "direct",
-        flops=4 * 640 * RA * HID2,
-        moved=4_000_000,
-        scratch=[pltpu.VMEM((ROWS, RA // 4), BF)],
-        limit=LARGE,
-    )(main, rest, gate_weight, up_weight)
     back_a = lax.all_to_all(to_send.reshape(NE, 8, RA + RA // 4), "expert", 0, 0, tiled=True)
     back_b = lax.all_to_all(summed.reshape(NE, 8, RB), "expert", 0, 0, tiled=True)
     part_a = call(combine_a_kernel, shape(NTOK, RA), "combine_a", flops=2 * ROWS * 128 * 2048)(

time: 231 us -> 226 us (0.978)
  blocking collectives: 114 us -> 164 us
  waiting for transfers between devices: 57.9 us -> 15.1 us
  Pallas kernels: 29.6 us -> 21.1 us
  starting transfers between devices: 12.5 us -> 9.08 us
    all_to_all x0 -> x1, blocking collectives: none -> 50 us  [per_device(): lax.all_to_all(send_a.reshape(NE, 8, SENT_A), 'expert', 0, 0, tiled=True)]
    all_gather x1, waiting for transfers between devices: 45.6 us -> 2.73 us  [per_device(): all_b = lax.all_gather(own_b, 'tensor', axis=0, tiled=True)]
    pallas_call x3 -> x1, Pallas kernels: 19.6 us -> 12.2 us  [per_device(): call(experts_kernel, (shape(NT, ROWS, RB), shape(ROWS, RA + RA // 4)), 'e...]
    all_to_all x1 -> x0, starting transfers between devices: 5.86 us -> none  [per_device(): lax.all_to_all(send_a.reshape(NE, 8, SENT_A), 'expert', 0, 0, tiled=True)]
    all_to_all x1, starting transfers between devices: 6.33 us -> 8.99 us  [per_device(): lax.all_to_all(summed.reshape(NE, 8, RB), 'expert', 0, 0, tiled=True)]
  transfers between devices with their start and end apart: 5 -> 4, of which waited for: 2 -> 2; matrix products, arithmetic and copies ran while one was open for 0% -> 0% of each run, Pallas kernels for 7% -> 2%
where the time goes in v3:
time: 226 us; the launch traced here: 225 us
  blocking collectives  164 us (73%)
  Pallas kernels  21.1 us (9%)
  waiting for transfers between devices  15.1 us (7%)
  between operations  13.2 us (6%)
  starting transfers between devices  9.08 us (4%)
  local copies, waits for them, and re-layouts  3.31 us (1%)
    all_to_all x1, blocking collectives, per_device(): lax.all_to_all(send_a.reshape(NE, 8, SENT_A), 'expert', 0, 0, tiled=True)  50 us
    all_to_all x1, blocking collectives, per_device(): lax.all_to_all(to_send.reshape(NE, 8, RA + RA // 4), 'expert', 0, 0, tile...  43.9 us
    all_to_all x1, blocking collectives, per_device(): lax.all_to_all(send_b.reshape(NE, 8, SENT_B), 'expert', 0, 0, tiled=True)  32.7 us
    all_to_all x1, blocking collectives, per_device(): msg = lax.all_to_all(msg, 'tensor', 0, 0, tiled=True).reshape(NTOK, lanes)  20.6 us
    all_to_all x1, blocking collectives, per_device(): lax.all_to_all(last.reshape(NT, PADDED, RA + RB), 'tensor', 0, 0, tiled=T...  16.5 us
    all_to_all x1, waiting for transfers between devices, per_device(): lax.all_to_all(summed.reshape(NE, 8, RB), 'expert', 0, 0, tiled=True)  12.3 us
    pallas_call x1, Pallas kernels, per_device(): call(experts_kernel, (shape(NT, ROWS, RB), shape(ROWS, RA + RA // 4)), 'e...  12.2 us
    all_to_all x1, starting transfers between devices, per_device(): lax.all_to_all(summed.reshape(NE, 8, RB), 'expert', 0, 0, tiled=True)  8.99 us
  transfers between devices with their start and end apart: 4, of which 2 were waited for; matrix products, arithmetic and copies ran while one was open for 0% of the time, Pallas kernels for 2%

profile of v3, /device:TPU:1, one launch (start us, length us, event | category | flops | bytes accessed | tf_op | source)
XLA Modules:
  0.0 225.5 jit_solution(4883754642799402666)
XLA Ops:
  6.5 1.8 start.1
  8.3 0.0 all-gather.3.cloned.1.call-update
  8.4 0.0 all-gather.5.cloned.1.call-start
  8.4 20.6 %all_to_all.30 = bf16[8,16,896]{2,1,0:T(8,128)(2,1)S(1)} all-to-all(bf16[8,16,896]{2,1,0:T(8,128)(2,1)} %get-tuple-element.11), channel_id=1, replica_groups=mesh['tensor'=8,'expert'=64] {'tensor'}, dimensions={0} | all-to-all | bytes 458752 | tf_op jit(solution)/shard_map/all_to_all | solution.py:412
  29.0 0.9 pack_b.1
  30.0 32.7 %all_to_all.31 = bf16[64,8,640]{2,1,0:T(8,128)(2,1)S(1)} all-to-all(bf16[64,8,640]{2,1,0:T(8,128)(2,1)S(1)} %bitcast.19), channel_id=1, replica_groups=mesh['tensor'=8,'expert'=64] {'expert'}, dimensions={0} | all-to-all | bytes 1310720 | tf_op jit(solution)/shard_map/all_to_all | solution.py:414
  62.6 1.5 unpack_b.1
  64.2 0.7 copy-done.1
  64.9 0.0 reduce-scatter.2.cloned.1.call-start
  65.0 0.0 all-gather.3.cloned.1.call-done.x_in
  65.0 1.3 copy-done
  66.3 1.9 pack_a.1
  68.3 50.0 %all_to_all.32 = bf16[64,8,1792]{2,1,0:T(8,128)(2,1)} all-to-all(bf16[64,8,1792]{2,1,0:T(8,128)(2,1)S(1)} %bitcast.12), channel_id=1, replica_groups=mesh['tensor'=8,'expert'=64] {'expert'}, dimensions={0} | all-to-all | bytes 3670016 | tf_op jit(solution)/shard_map/all_to_all | solution.py:432
  118.3 2.7 %all-gather.5.cloned.1.call-done.b_in = bf16[4608,512]{1,0:T(8,128)(2,1)} async-done(((bf16[576,512]{1,0:T(8,128)(2,1)}), bf16[4608,512]{1,0:T(8,128)(2,1)}) %all-gather.5.cloned.1.call-update) | async-done | bytes 4718608 | tf_op jit(solution)/shard_map/all_gather | solution.py:423
  121.0 12.2 %experts.1 = (bf16[8,512,256]{2,1,0:T(8,128)(2,1)}, bf16[512,1280]{1,0:T(8,128)(2,1)}) custom-call(bf16[512,1792]{1,0:T(8,128)(2,1)} %bitcast.22, bf16[4608,512]{1,0:T(8,128)(2,1)} %all-gather.5.cloned.1.call-done.b_in, f32[640,128]{1,0:T(8,128)} %copy-done.1, bf16[2,96,2560]{2,1,0:T(8,128)(2,1)} %wg_in.1, bf16[2,96,2560]{2,1,0:T(8,128)(2,1)} %wu_in.1, ...), custom_call_target="tpu_custom_call" | custom-call | flops 3145728000 | bytes 13000000 | tf_op jit(solution)/shard_map/experts/pallas_call | solution.py:433
  133.2 0.0 reduce-scatter.2.cloned.1.call-update
  133.2 1.3 copy-done.2
  134.5 43.9 %all_to_all.33 = bf16[64,8,1280]{2,1,0:T(8,128)(2,1)S(1)} all-to-all(bf16[64,8,1280]{2,1,0:T(8,128)(2,1)S(1)} %bitcast.23), channel_id=1, replica_groups=mesh['tensor'=8,'expert'=64] {'expert'}, dimensions={0} | all-to-all | bytes 2621440 | tf_op jit(solution)/shard_map/all_to_all | solution.py:457
  178.5 9.0 %all-to-all-start.3 = ((bf16[64,8,256]{2,1,0:T(8,128)(2,1)}), bf16[64,8,256]{2,1,0:T(8,128)(2,1)S(1)}, u32[]{:S(2)}, u32[]{:S(2)}) async-start(bf16[64,8,256]{2,1,0:T(8,128)(2,1)} %bitcast.24), calls=%async_computation.4 | async-start | bytes 524288 | tf_op jit(solution)/shard_map/all_to_all | solution.py:458
  187.5 0.9 combine_a.1.a_ref
  188.4 12.3 %all-to-all-done.3 = bf16[64,8,256]{2,1,0:T(8,128)(2,1)S(1)} async-done(((bf16[64,8,256]{2,1,0:T(8,128)(2,1)}), bf16[64,8,256]{2,1,0:T(8,128)(2,1)S(1)}, u32[]{:S(2)}, u32[]{:S(2)}) %all-to-all-start.3) | async-done | bytes 262176 | tf_op jit(solution)/shard_map/all_to_all | solution.py:458
  200.6 1.1 combine_b.1
  201.8 16.5 %all_to_all.34.in_ref = bf16[8,16,1280]{2,1,0:T(8,128)(2,1)S(1)} all-to-all(bf16[8,16,1280]{2,1,0:T(8,128)(2,1)S(1)} %bitcast.20), channel_id=1, replica_groups=mesh['tensor'=8,'expert'=64] {'tensor'}, dimensions={0} | all-to-all | bytes 655360 | tf_op jit(solution)/shard_map/all_to_all | solution.py:465
  218.3 0.7 finish.1
  (6 shorter events, 0.0 us)
Async XLA Ops:
  6.5 58.4 %all-gather.3.cloned.1.call-start = ((), (), s32[]{:S(2)}) async-start(), calls=%async_computation.7 | async-start | bytes 1474560 | tf_op jit(solution)/shard_map/all_gather | solution.py:411
  8.4 112.7 %all-gather.5.cloned.1.call-start = ((), (), s32[]{:S(2)}) async-start(), calls=%async_computation.8 | async-start | bytes 5308416 | tf_op jit(solution)/shard_map/all_gather | solution.py:423
  64.2 0.7 copy-start.1
  64.9 113.6 %reduce-scatter.2.cloned.1.call-start = ((), (), s32[]{:S(2)}) async-start(), calls=%async_computation.9 | async-start | bytes 2359296 | tf_op jit(solution)/shard_map/reduce_scatter | solution.py:456
  65.0 1.3 copy-start
  133.2 1.3 copy-start.2
  178.5 22.2 %all-to-all-start.3 = ((bf16[64,8,256]{2,1,0:T(8,128)(2,1)}), bf16[64,8,256]{2,1,0:T(8,128)(2,1)S(1)}, u32[]{:S(2)}, u32[]{:S(2)}) async-start(bf16[64,8,256]{2,1,0:T(8,128)(2,1)} %bitcast.24), calls=%async_computation.4 | async-start | bytes 524288 | tf_op jit(solution)/shard_map/all_to_all | solution.py:458
Sparse Core Ops, SparseCore 0:
  9.4 43.6 all-gather.2
  65.0 55.9 all-gather.4
  133.3 39.7 reduce-scatter.1

commit v4 on v3

--- a/solution.py
+++ b/solution.py
@@ -26,6 +26,9 @@
 GATHERED = ROWS + NE
 RA = 1024
 RB = 256
+BACK_A = RA + 128
+LAST = RA + RB
+LAST_PACKED = LAST * 3 // 2
 SMALL = 24 * 1024 * 1024
 LARGE = 60 * 1024 * 1024
 
@@ -209,7 +212,7 @@
     wu_in,
     wd_in,
     rs_out,
-    send_ref,
+    send_out,
     a_ref,
     b_ref,
     gates_ref,
@@ -219,23 +222,46 @@
     left_ref,
     z_ref,
     rs_ref,
+    send_ref,
     sems,
     out_sems,
 ):
-    pairs = [(wg_in, wg_ref), (wu_in, wu_ref), (wd_in, wd_ref), (a_in, a_ref), (gates_in, gates_ref)]
-    for t in (0, 4, 1, 5, 2, 6, 3, 7):
-        rows = pl.ds(GATHERED * t, GATHERED)
-        pairs.append((b_in.at[rows], b_ref.at[rows]))
-    copies = [pltpu.make_async_copy(src, dst, sems.at[i]) for i, (src, dst) in enumerate(pairs)]
-    for copy in copies:
-        copy.start()
+    started = []
+
+    def fetch(src, dst, parts):
+        copies = []
+        for part in parts:
+            copies.append(pltpu.make_async_copy(src.at[part], dst.at[part], sems.at[len(started)]))
+            copies[-1].start()
+            started.append(copies[-1])
+        return copies
+
+    def fetch_weights(low):
+        part = (slice(None), slice(None), pl.ds(low, 512))
+        return [
+            copy
+            for src, dst in ((wg_in, wg_ref), (wu_in, wu_ref), (wd_in, wd_ref))
+            for copy in fetch(src, dst, [part])
+        ]
+
+    def arrive(copies):
+        for copy in copies:
+            copy.wait()
+
+    every = slice(None)
+    left_copies = fetch(
+        a_in, a_ref, [(pl.ds(256 * h, 256), pl.ds(2 * FA, SENT_A - 2 * FA)) for h in range(2)]
+    )
+    main_copies = fetch(a_in, a_ref, [(every, pl.ds(FA * i, FA)) for i in range(2)]) + fetch_weights(0)
+    b_copies = [
+        fetch(b_in, b_ref, [pl.ds(GATHERED * u + 288 * i, 288) for u in (t, t + 4) for i in range(2)])
+        + fetch_weights(FA + FB * t)
+        for t in range(4)
+    ]
+    g_copies = fetch(gates_in, gates_ref, [pl.ds(0, ROWS + 128)])
     turn = perm(False)
     turn_back = perm(True)
-    for copy in copies[:4]:
-        copy.wait()
-    wg = wg_ref[...].reshape(HID2, D)
-    wu = wu_ref[...].reshape(HID2, D)
-    wd = wd_ref[...].reshape(HID2, D)
+    arrive(left_copies)
     for h in range(2):
         turned = dot(turn, a_ref[256 * h : 256 * (h + 1), 2 * FA : SENT_A]).astype(BF)
         for q in range(2 * LA // 512):
@@ -246,29 +272,47 @@
                     left_ref[low : low + 32, base + 128 * k : base + 128 * (k + 1)] = turned[
                         32 * (4 * s + k) : 32 * (4 * s + k + 1), 128 * q : 128 * (q + 1)
                     ]
-    gate_pre = dot_t(a_ref[:, 0:FA], wg[:, 0:FA])
-    up_pre = dot_t(a_ref[:, 0:FA], wu[:, 0:FA])
-    back_proj = dot_t(a_ref[:, FA : 2 * FA], wd[:, 0:FA])
-    copies[4].wait()
+    arrive(main_copies)
+
+    def block(ref, low):
+        return ref[:, :, low : low + 512].reshape(HID2, 512)
+
+    def add_left(sums, low):
+        rows = left_ref[:, low : low + 512]
+        products = (
+            dot_t(rows, block(wg_ref, low)),
+            dot_t(rows, block(wu_ref, low)),
+            dot_t(left_ref[:, D + low : D + low + 512], block(wd_ref, low)),
+        )
+        return [a + b for a, b in zip(sums, products)]
+
+    left_sums = add_left([0.0] * 3, 0)
+    gate_pre = dot_t(a_ref[:, 0:FA], block(wg_ref, 0))
+    up_pre = dot_t(a_ref[:, 0:FA], block(wu_ref, 0))
+    back_proj = dot_t(a_ref[:, FA : 2 * FA], block(wd_ref, 0))
     for t in range(4):
-        copies[5 + 2 * t].wait()
-        copies[6 + 2 * t].wait()
-        cols = slice(FA + FB * t, FA + FB * (t + 1))
+        arrive(b_copies[t])
+        low = FA + FB * t
         x0, y0 = GATHERED * t, GATHERED * (t + 4)
         rows = b_ref[x0 : x0 + ROWS, :]
-        gate_pre = gate_pre + dot_t(rows, wg[:, cols])
-        up_pre = up_pre + dot_t(rows, wu[:, cols])
-        back_proj = back_proj + dot_t(b_ref[y0 : y0 + ROWS, :], wd[:, cols])
+        gate_pre = gate_pre + dot_t(rows, block(wg_ref, low))
+        up_pre = up_pre + dot_t(rows, block(wu_ref, low))
+        back_proj = back_proj + dot_t(b_ref[y0 : y0 + ROWS, :], block(wd_ref, low))
         for base, start in ((0, x0), (D, y0)):
             low = base + LA + LB * t
             for s in range(2):
                 left_ref[64 * s : 64 * s + 64, low : low + LB] = b_ref[
                     start + ROWS : start + GATHERED, LB * s : LB * (s + 1)
                 ]
+        if FA + FB * (t + 1) <= LA:
+            left_sums = add_left(left_sums, FA + FB * t)
+    arrive(g_copies)
+    wg = wg_ref[...].reshape(HID2, D)
+    wu = wu_ref[...].reshape(HID2, D)
+    for low in range(LA, D, 512):
+        left_sums = add_left(left_sums, low)
     gate_left, up_left = grads(
-        dot_t(left_ref[:, 0:D], wg),
-        dot_t(left_ref[:, 0:D], wu),
-        dot_t(left_ref[:, D : 2 * D], wd),
+        *left_sums,
         (gates_ref[ROWS : ROWS + 128, 0:1], gates_ref[ROWS : ROWS + 128, 1:2]),
     )
     gate_grad, up_grad = grads(
@@ -282,15 +326,29 @@
             dot(gate_left, wg[:, cols]) + dot(up_left, wu[:, cols]),
         )
 
+    outs = []
+    rests = []
+    for q in range(RA // 512):
+        sums, rest = part(512 * q, 512)
+        send_ref[:, 512 * q : 512 * (q + 1)] = sums.astype(BF)
+        rests.append(rest.astype(BF))
+    for h in range(2):
+        for s in range(2):
+            for k in range(4):
+                low = 256 * h + 32 * (4 * s + k)
+                z_ref[low : low + 32, :] = rests[1][64 * s + 32 * h : 64 * s + 32 * h + 32, 128 * k : 128 * (k + 1)]
+        rows = slice(256 * h, 256 * (h + 1))
+        send_ref[rows, RA:BACK_A] = dot(turn_back, z_ref[rows, :]).astype(BF)
+        for i in range(2 * h, 2 * h + 2):
+            rows = pl.ds(128 * i, 128)
+            outs.append(pltpu.make_async_copy(send_ref.at[rows], send_out.at[rows], out_sems.at[NT + i]))
+            outs[-1].start()
     row = iota((256, 256), 0)
     col = iota((256, 256), 1)
     place_main = mask(((col >> 3) == (row >> 3)) & (((col & 7) >> 1) == (row & 7)))
     row = iota((ROWS, 256), 0)
     col = iota((ROWS, 256), 1)
-    sub = row & 7
-    slot = col >> 6
-    fits = ((slot < 2) & (sub == 4 + slot)) | ((slot >= 2) & (sub == 6))
-    place_left = mask(((col & 63) == (row >> 3)) & fits)
+    place_left = mask(((col & 63) == (row >> 3)) & ((row & 7) == 4 + (col >> 6)))
 
     def halves(tile, odd_rows, odd_slice):
         low_half = iota(tile.shape, 1) < 64
@@ -300,7 +358,6 @@
 
     odd_main = (iota((ROWS, 128), 0) & 1) == 1
     odd_left = iota((128, 128), 0) >= 64
-    outs = []
     for c in range(2):
         half_main, half_left = part(2048 + 256 * c, 256)
         for pair in range(2):
@@ -309,10 +366,16 @@
             tile_main = half_main[:, 128 * pair : 128 * (pair + 1)]
             tile_left = half_left[:, 128 * pair : 128 * (pair + 1)]
             mains = jnp.concatenate([halves(tile_main, odd_main, i == 1) for i in range(2)], axis=1)
+            halves_left = [halves(tile_left, odd_left, i == 1) for i in range(2)]
+            extra = [
+                rests[0][64 * (t // 4) : 64 * (t // 4) + 64, 128 * (t % 4) : 128 * (t % 4 + 1)]
+                for t in (t0, t0 + 1)
+            ]
             lefts = jnp.concatenate(
                 [
                     full_left.astype(BF),
-                    jnp.concatenate([halves(tile_left, odd_left, i == 1) for i in range(2)], axis=1),
+                    jnp.concatenate([half[0:64] + half[64:128] for half in halves_left], axis=1),
+                    jnp.concatenate(extra, axis=1),
                 ],
                 axis=0,
             )
@@ -326,20 +389,6 @@
                 rs_ref[t0 + i, :, 0:128] = full_main[:, 128 * i : 128 * (i + 1)].astype(BF)
                 outs.append(pltpu.make_async_copy(rs_ref.at[t0 + i], rs_out.at[t0 + i], out_sems.at[t0 + i]))
                 outs[-1].start()
-    for q in range(RA // 512):
-        sums, rest = part(512 * q, 512)
-        send_ref[:, 512 * q : 512 * (q + 1)] = sums.astype(BF)
-        rest = rest.astype(BF)
-        for h in range(2):
-            for s in range(2):
-                for k in range(4):
-                    low = 32 * (4 * s + k)
-                    z_ref[256 * h + low : 256 * h + low + 32, 128 * q : 128 * (q + 1)] = rest[
-                        64 * s + 32 * h : 64 * s + 32 * h + 32, 128 * k : 128 * (k + 1)
-                    ]
-    for h in range(2):
-        rows = slice(256 * h, 256 * (h + 1))
-        send_ref[rows, RA : RA + RA // 4] = dot(turn_back, z_ref[rows, :]).astype(BF)
     for copy in outs:
         copy.wait()
 
@@ -356,46 +405,67 @@
     spread, sub = spread_positions(msg_ref)
     main = mask(spread == sub)
     total = dot(main, a_ref[:, 0:RA])
+    out_ref[:, 0:512] = total[:, 0:512].astype(BF)
     for k in range(4):
         left = mask((spread == 8 + (sub >> 2)) & ((sub & 3) == k))
-        rest = dot(left, a_ref[:, RA : RA + RA // 4])
-        for q in range(RA // 512):
-            low = 512 * q + 128 * k
-            out_ref[:, low : low + 128] = (
-                total[:, low : low + 128] + rest[:, 128 * q : 128 * (q + 1)]
-            ).astype(BF)
-
-
-def combine_b_kernel(msg_ref, b_ref, a_ref, out_ref):
+        low = 512 + 128 * k
+        rest = dot(left, a_ref[:, RA:BACK_A])
+        out_ref[:, low : low + 128] = (total[:, low : low + 128] + rest).astype(BF)
+
+
+def combine_b_kernel(msg_ref, b_ref, a_ref, slice_ref, out_ref):
     spread, sub = spread_positions(msg_ref)
-    out_ref[:, 0:RA] = a_ref[...]
     main = mask(spread == sub)
     tile = b_ref[:, 128:256]
     rest = mask(((sub == 4) & (spread == 8)) | ((sub == 5) & (spread == 9)))
-    out_ref[:, RA : RA + 128] = (dot(main, b_ref[:, 0:128]) + dot(rest, tile)).astype(BF)
+    full = dot(main, b_ref[:, 0:128]) + dot(rest, tile)
     low = dot(mask(((sub < 4) & (spread == 2 * sub)) | ((sub == 6) & (spread == 8))), tile)
     high = dot(mask(((sub < 4) & (spread == 2 * sub + 1)) | ((sub == 6) & (spread == 9))), tile)
     both = jnp.where(iota((NTOK, 128), 1) < 64, low, high)
-    out_ref[:, RA + 128 : RA + 256] = (both + pltpu.roll(both, 64, 1)).astype(BF)
+    both = both + pltpu.roll(both, 64, 1)
+    me = slice_ref[0, 0]
+    extra = dot(mask((sub == 7) & (spread == 8 + (me >> 2))), tile)
+    tiles = [
+        a_ref[:, 128 * j : 128 * (j + 1)].astype(F32) + jnp.where((me & 3) == j, extra, 0.0)
+        for j in range(4)
+    ]
+    tiles += [a_ref[:, 512:RA].astype(F32), full, both]
+    values = jnp.concatenate([tile.astype(BF) for tile in tiles], axis=1)
+    row = iota((64, NTOK), 0)
+    col = iota((64, NTOK), 1)
+    out_ref[:, 0:LAST] = dot(mask(col == 16 * (row >> 3) + (row & 7)), values).astype(BF)
+    spread = [
+        dot(mask((col == 16 * (row >> 3) + 8 + (row & 3)) & (((row >> 2) & 1) == i)), values)
+        for i in range(2)
+    ]
+    for j in range(LAST // 256):
+        packed = spread[0][:, 256 * j : 256 * j + 128] + spread[1][:, 256 * j + 128 : 256 * (j + 1)]
+        out_ref[:, LAST + 128 * j : LAST + 128 * (j + 1)] = packed.astype(BF)
 
 
 def finish_kernel(in_ref, out_ref):
-    total = in_ref[0, :, 0:RA].astype(F32)
-    for t in range(1, NT):
-        total = total + in_ref[t, :, 0:RA].astype(F32)
-    out_ref[:, 0:RA] = total.astype(BF)[0:OWN]
+    def tile(t, j):
+        first = in_ref[t, :, 128 * j : 128 * (j + 1)].astype(F32)
+        low = LAST + 128 * (j // 2)
+        rest = in_ref[t, :, low : low + 128].astype(F32)
+        return first, rest
+
+    def store(low, first, rest, odd):
+        rest = pltpu.roll(rest, 4, 0) if odd else rest
+        out_ref[:, low : low + 128] = jnp.concatenate([first, rest], axis=0).astype(BF)[0:OWN]
+
+    for j in range(RA // 128):
+        first, rest = tile(0, j)
+        for t in range(1, NT):
+            more = tile(t, j)
+            first, rest = first + more[0], rest + more[1]
+        store(128 * j, first, rest, j % 2 == 1)
     for t in range(NT):
-        low = RA + 128 * t
-        out_ref[:, low : low + 128] = in_ref[t, 0:OWN, RA : RA + 128]
-    low_half = iota((PADDED, 128), 1) < 64
+        store(RA + 128 * t, *tile(t, RA // 128), False)
+    low_half = iota((8, 128), 1) < 64
     for t in range(0, NT, 2):
-        low = 2048 + 64 * t
-        tile = jnp.where(
-            low_half,
-            in_ref[t, :, RA + 128 : RA + 256].astype(F32),
-            in_ref[t + 1, :, RA + 128 : RA + 256].astype(F32),
-        )
-        out_ref[:, low : low + 128] = tile.astype(BF)[0:OWN]
+        pair = zip(tile(t, RA // 128 + 1), tile(t + 1, RA // 128 + 1))
+        store(2048 + 64 * t, *[jnp.where(low_half, one, two) for one, two in pair], True)
 
 
 def shape(*dims, dtype=BF):
@@ -432,7 +502,7 @@
     recv_a = lax.all_to_all(send_a.reshape(NE, 8, SENT_A), "expert", 0, 0, tiled=True)
     to_sum, to_send = call(
         experts_kernel,
-        (shape(NT, ROWS, RB), shape(ROWS, RA + RA // 4)),
+        (shape(NT, ROWS, RB), shape(ROWS, BACK_A)),
         "experts",
         flops=10 * 640 * D * HID2,
         moved=13_000_000,
@@ -444,25 +514,31 @@
             pltpu.VMEM((2, HID2 // 2, D), BF),
             pltpu.VMEM((2, HID2 // 2, D), BF),
             pltpu.VMEM((128, 2 * D), BF),
-            pltpu.VMEM((ROWS, RA // 4), BF),
+            pltpu.VMEM((ROWS, 128), BF),
             pltpu.VMEM((NT, ROWS, RB), BF),
-            pltpu.SemaphoreType.DMA((5 + NT,)),
-            pltpu.SemaphoreType.DMA((NT,)),
+            pltpu.VMEM((ROWS, BACK_A), BF),
+            pltpu.SemaphoreType.DMA((36,)),
+            pltpu.SemaphoreType.DMA((NT + 4,)),
         ],
         limit=LARGE,
         ins=[HBM] * 6,
-        outs=(HBM, VMEM),
+        outs=(HBM, HBM),
     )(recv_a.reshape(ROWS, SENT_A), all_b, gates, *weights)
     summed = lax.psum_scatter(to_sum, "tensor", scatter_dimension=0, tiled=False)
-    back_a = lax.all_to_all(to_send.reshape(NE, 8, RA + RA // 4), "expert", 0, 0, tiled=True)
+    back_a = lax.all_to_all(to_send.reshape(NE, 8, BACK_A), "expert", 0, 0, tiled=True)
     back_b = lax.all_to_all(summed.reshape(NE, 8, RB), "expert", 0, 0, tiled=True)
     part_a = call(combine_a_kernel, shape(NTOK, RA), "combine_a", flops=2 * ROWS * 128 * 2048)(
-        msg, back_a.reshape(ROWS, RA + RA // 4)
-    )
-    last = call(combine_b_kernel, shape(NTOK, RA + RB), "combine_b", flops=2 * ROWS * 128 * 512)(
-        msg, back_b.reshape(ROWS, RB), part_a
-    )
-    last = lax.all_to_all(last.reshape(NT, PADDED, RA + RB), "tensor", 0, 0, tiled=True)
+        msg, back_a.reshape(ROWS, BACK_A)
+    )
+    me = lax.axis_index("tensor").astype(I32).reshape(1, 1)
+    last = call(
+        combine_b_kernel,
+        shape(64, LAST_PACKED),
+        "combine_b",
+        flops=2 * ROWS * 128 * 1024,
+        ins=[VMEM, VMEM, VMEM, pl.BlockSpec(memory_space=pltpu.SMEM)],
+    )(msg, back_b.reshape(ROWS, RB), part_a, me)
+    last = lax.all_to_all(last.reshape(NT, 8, LAST_PACKED), "tensor", 0, 0, tiled=True)
     return call(finish_kernel, shape(OWN, D), "finish")(last)
 
 

time: 226 us -> 223 us (0.987)
  blocking collectives: 164 us -> 159 us
  starting transfers between devices: 9.08 us -> 12 us
    all_to_all x2, blocking collectives: 60.4 us -> 56.1 us  [the longest x1 40.9 us: per_device(): lax.all_to_all(to_send.reshape(NE, 8, BACK_A), 'expert', 0, 0, tiled=True)]
    all_to_all x1, starting transfers between devices: 8.99 us -> 11.9 us  [per_device(): lax.all_to_all(summed.reshape(NE, 8, RB), 'expert', 0, 0, tiled=True)]
where the time goes in v4:
time: 223 us
  blocking collectives  159 us (71%)
  Pallas kernels  19.7 us (9%)
  waiting for transfers between devices  15.1 us (7%)
  between operations  13.2 us (6%)
  starting transfers between devices  12 us (5%)
  local copies, waits for them, and re-layouts  3.26 us (1%)
    all_to_all x1, blocking collectives, per_device(): lax.all_to_all(send_a.reshape(NE, 8, SENT_A), 'expert', 0, 0, tiled=True)  50 us
    all_to_all x1, blocking collectives, per_device(): lax.all_to_all(to_send.reshape(NE, 8, BACK_A), 'expert', 0, 0, tiled=True)  40.9 us
    all_to_all x1, blocking collectives, per_device(): lax.all_to_all(send_b.reshape(NE, 8, SENT_B), 'expert', 0, 0, tiled=True)  32.7 us
    all_to_all x1, blocking collectives, per_device(): msg = lax.all_to_all(msg, 'tensor', 0, 0, tiled=True).reshape(NTOK, lanes)  20.6 us
    all_to_all x1, blocking collectives, per_device(): lax.all_to_all(last.reshape(NT, 8, LAST_PACKED), 'tensor', 0, 0, tiled=True)  15.2 us
    all_to_all x1, waiting for transfers between devices, per_device(): lax.all_to_all(summed.reshape(NE, 8, RB), 'expert', 0, 0, tiled=True)  12.3 us
    all_to_all x1, starting transfers between devices, per_device(): lax.all_to_all(summed.reshape(NE, 8, RB), 'expert', 0, 0, tiled=True)  11.9 us
    pallas_call x1, Pallas kernels, per_device(): call(experts_kernel, (shape(NT, ROWS, RB), shape(ROWS, BACK_A)), 'experts...  10.5 us
  transfers between devices with their start and end apart: 4, of which 2 were waited for; matrix products, arithmetic and copies ran while one was open for 0% of the time, Pallas kernels for 2%

profile of v4, /device:TPU:1, one launch (start us, length us, event | category | flops | bytes accessed | tf_op | source)
XLA Modules:
  0.0 222.6 jit_solution(3657336685400385344)
XLA Ops:
  6.5 1.8 start.1
  8.3 0.0 all-gather.3.cloned.1.call-update
  8.4 0.0 all-gather.5.cloned.1.call-start
  8.4 20.6 %all_to_all.30 = bf16[8,16,896]{2,1,0:T(8,128)(2,1)S(1)} all-to-all(bf16[8,16,896]{2,1,0:T(8,128)(2,1)} %get-tuple-element.11), channel_id=1, replica_groups=mesh['tensor'=8,'expert'=64] {'tensor'}, dimensions={0} | all-to-all | bytes 458752 | tf_op jit(solution)/shard_map/all_to_all | solution.py:482
  29.0 0.9 pack_b.1
  30.0 32.7 %all_to_all.31 = bf16[64,8,640]{2,1,0:T(8,128)(2,1)S(1)} all-to-all(bf16[64,8,640]{2,1,0:T(8,128)(2,1)S(1)} %bitcast.20), channel_id=1, replica_groups=mesh['tensor'=8,'expert'=64] {'expert'}, dimensions={0} | all-to-all | bytes 1310720 | tf_op jit(solution)/shard_map/all_to_all | solution.py:484
  62.6 1.5 unpack_b.1
  64.2 0.7 copy-done.1
  64.9 0.0 reduce-scatter.2.cloned.1.call-start
  65.0 0.0 all-gather.3.cloned.1.call-done.x_in
  65.0 1.3 copy-done
  66.3 1.9 pack_a.1
  68.3 50.0 %all_to_all.32 = bf16[64,8,1792]{2,1,0:T(8,128)(2,1)} all-to-all(bf16[64,8,1792]{2,1,0:T(8,128)(2,1)S(1)} %bitcast.13), channel_id=1, replica_groups=mesh['tensor'=8,'expert'=64] {'expert'}, dimensions={0} | all-to-all | bytes 3670016 | tf_op jit(solution)/shard_map/all_to_all | solution.py:502
  118.3 2.7 %all-gather.5.cloned.1.call-done.b_in = bf16[4608,512]{1,0:T(8,128)(2,1)} async-done(((bf16[576,512]{1,0:T(8,128)(2,1)}), bf16[4608,512]{1,0:T(8,128)(2,1)}) %all-gather.5.cloned.1.call-update) | async-done | bytes 4718608 | tf_op jit(solution)/shard_map/all_gather | solution.py:493
  121.0 10.5 %experts.1 = (bf16[8,512,256]{2,1,0:T(8,128)(2,1)}, bf16[512,1152]{1,0:T(8,128)(2,1)}) custom-call(bf16[512,1792]{1,0:T(8,128)(2,1)} %bitcast.23, bf16[4608,512]{1,0:T(8,128)(2,1)} %all-gather.5.cloned.1.call-done.b_in, f32[640,128]{1,0:T(8,128)} %copy-done.1, bf16[2,96,2560]{2,1,0:T(8,128)(2,1)} %wg_in.1, bf16[2,96,2560]{2,1,0:T(8,128)(2,1)} %wu_in.1, ...), custom_call_target="tpu_custom_call" | custom-call | flops 3145728000 | bytes 13000000 | tf_op jit(solution)/shard_map/experts/pallas_call | solution.py:503
  131.6 0.0 reduce-scatter.2.cloned.1.call-update
  131.6 1.2 copy-done.2
  132.8 40.9 %all_to_all.33 = bf16[64,8,1152]{2,1,0:T(8,128)(2,1)S(1)} all-to-all(bf16[64,8,1152]{2,1,0:T(8,128)(2,1)S(1)} %bitcast.24), channel_id=1, replica_groups=mesh['tensor'=8,'expert'=64] {'expert'}, dimensions={0} | all-to-all | bytes 2359296 | tf_op jit(solution)/shard_map/all_to_all | solution.py:528
  173.8 11.9 %all-to-all-start.3 = ((bf16[64,8,256]{2,1,0:T(8,128)(2,1)}), bf16[64,8,256]{2,1,0:T(8,128)(2,1)S(1)}, u32[]{:S(2)}, u32[]{:S(2)}) async-start(bf16[64,8,256]{2,1,0:T(8,128)(2,1)} %bitcast.25), calls=%async_computation.4 | async-start | bytes 524288 | tf_op jit(solution)/shard_map/all_to_all | solution.py:529
  185.7 0.9 combine_a.1.a_ref
  186.6 12.3 %all-to-all-done.3 = bf16[64,8,256]{2,1,0:T(8,128)(2,1)S(1)} async-done(((bf16[64,8,256]{2,1,0:T(8,128)(2,1)}), bf16[64,8,256]{2,1,0:T(8,128)(2,1)S(1)}, u32[]{:S(2)}, u32[]{:S(2)}) %all-to-all-start.3) | async-done | bytes 262176 | tf_op jit(solution)/shard_map/all_to_all | solution.py:529
  198.8 1.4 combine_b.1
  200.2 15.2 %all_to_all.34.in_ref = bf16[8,8,1920]{2,1,0:T(8,128)(2,1)S(1)} all-to-all(bf16[8,8,1920]{2,1,0:T(8,128)(2,1)S(1)} %bitcast.22), channel_id=1, replica_groups=mesh['tensor'=8,'expert'=64] {'tensor'}, dimensions={0} | all-to-all | bytes 491520 | tf_op jit(solution)/shard_map/all_to_all | solution.py:541
  215.4 0.7 finish.1
  (6 shorter events, 0.0 us)
Async XLA Ops:
  6.5 58.4 %all-gather.3.cloned.1.call-start = ((), (), s32[]{:S(2)}) async-start(), calls=%async_computation.7 | async-start | bytes 1474560 | tf_op jit(solution)/shard_map/all_gather | solution.py:481
  8.4 112.7 %all-gather.5.cloned.1.call-start = ((), (), s32[]{:S(2)}) async-start(), calls=%async_computation.8 | async-start | bytes 5308416 | tf_op jit(solution)/shard_map/all_gather | solution.py:493
  64.2 0.7 copy-start.1
  64.9 108.9 %reduce-scatter.2.cloned.1.call-start = ((), (), s32[]{:S(2)}) async-start(), calls=%async_computation.9 | async-start | bytes 2359296 | tf_op jit(solution)/shard_map/reduce_scatter | solution.py:527
  65.0 1.3 copy-start
  131.6 1.3 copy-start.2
  173.8 25.1 %all-to-all-start.3 = ((bf16[64,8,256]{2,1,0:T(8,128)(2,1)}), bf16[64,8,256]{2,1,0:T(8,128)(2,1)S(1)}, u32[]{:S(2)}, u32[]{:S(2)}) async-start(bf16[64,8,256]{2,1,0:T(8,128)(2,1)} %bitcast.25), calls=%async_computation.4 | async-start | bytes 524288 | tf_op jit(solution)/shard_map/all_to_all | solution.py:529
Sparse Core Ops, SparseCore 0:
  9.4 43.6 all-gather.2
  65.0 55.9 all-gather.4
  131.7 39.7 reduce-scatter.1

commit v5 on v4

--- a/solution.py
+++ b/solution.py
@@ -142,13 +142,19 @@
     out_ref[:, FB : FB + 128] = jnp.where(sub < 4, tile, dot_t(pick, gate_of)).astype(BF)
 
 
-def unpack_b_kernel(in_ref, out_ref, gate_out, gate_ref, sem):
+def unpack_b_kernel(in_ref, out_ref):
     out_ref[0:ROWS, :] = in_ref[:, 0:FB]
-    turn = perm(False)
-    turned = [dot(turn, in_ref[256 * h : 256 * (h + 1), FB : FB + 128]) for h in range(2)]
-    turned = jnp.concatenate([turned[h][32 * r : 32 * (r + 1)] for r in range(6) for h in range(2)], axis=0)
-    for r in range(4):
-        out_ref[ROWS : ROWS + 64, 128 * r : 128 * (r + 1)] = turned[64 * r : 64 * (r + 1)].astype(BF)
+    turn = perm(False)[0:128]
+    for h in range(2):
+        turned = dot(turn, in_ref[256 * h : 256 * (h + 1), FB : FB + 128]).astype(BF)
+        for r in range(4):
+            low = ROWS + 32 * h
+            out_ref[low : low + 32, 128 * r : 128 * (r + 1)] = turned[32 * r : 32 * (r + 1)]
+
+
+def gates_as_columns(tile_ref, gate_ref):
+    turn = perm(False)[128:192]
+    turned = [dot(turn, tile_ref[256 * h : 256 * (h + 1), :]) for h in range(2)]
     spread = mask((iota((ROWS, 64), 0) >> 3) == iota((ROWS, 64), 1))
     wide = iota((ROWS, 128), 1)
     sub = iota((ROWS, 128), 0) & 7
@@ -156,21 +162,19 @@
     rest = jnp.zeros((128, 128), F32)
     lane = iota((128, 128), 1)
     for e in range(2):
-        own = turned[64 * (4 + e) : 64 * (5 + e)]
+        own = jnp.concatenate([part[32 * e : 32 * (e + 1)] for part in turned], axis=0)
         both = jnp.where(wide == sub, dot(spread, own.astype(BF)), 0.0)
         main = jnp.where(wide == e, jnp.sum(both, axis=1, keepdims=True), main)
         column = jnp.concatenate([own[:, 8:9], own[:, 9:10]], axis=0)
         rest = jnp.where(lane == e, column, rest)
     gate_ref[0:ROWS, :] = main
     gate_ref[ROWS : ROWS + 128, :] = rest
-    copy = pltpu.make_async_copy(gate_ref, gate_out, sem)
-    copy.start()
-    copy.wait()
-
-
-def pack_a_kernel(msg_ref, x_in, out_ref, x_ref, sem):
+
+
+def pack_a_kernel(msg_ref, tile_ref, x_in, out_ref, gate_ref, x_ref, sem):
     copy = pltpu.make_async_copy(x_in, x_ref, sem)
     copy.start()
+    gates_as_columns(tile_ref, gate_ref)
     pos, _ = positions(msg_ref[:, FB + LB : FB + LB + META])
     main, left = one_hots(pos)
     sub4 = iota((ROWS, 128), 0) & 3
@@ -482,23 +486,17 @@
     msg = lax.all_to_all(msg, "tensor", 0, 0, tiled=True).reshape(NTOK, lanes)
     send_b = call(pack_b_kernel, shape(ROWS, SENT_B), "pack_b", flops=2 * ROWS * 128 * 1280)(msg)
     recv_b = lax.all_to_all(send_b.reshape(NE, 8, SENT_B), "expert", 0, 0, tiled=True)
-    own_b, gates = call(
-        unpack_b_kernel,
-        (shape(GATHERED, FB), shape(ROWS + 128, 128, dtype=F32)),
-        "unpack_b",
-        flops=2 * ROWS * ROWS * 128,
-        scratch=[pltpu.VMEM((ROWS + 128, 128), F32), pltpu.SemaphoreType.DMA],
-        outs=(VMEM, HBM),
-    )(recv_b.reshape(ROWS, SENT_B))
+    recv_b = recv_b.reshape(ROWS, SENT_B)
+    own_b = call(unpack_b_kernel, shape(GATHERED, FB), "unpack_b", flops=2 * ROWS * 256 * 128)(recv_b)
     all_b = lax.all_gather(own_b, "tensor", axis=0, tiled=True)
-    send_a = call(
+    send_a, gates = call(
         pack_a_kernel,
-        shape(ROWS, SENT_A),
+        (shape(ROWS, SENT_A), shape(ROWS + 128, 128, dtype=F32)),
         "pack_a",
         flops=2 * ROWS * 128 * 4096,
         scratch=[pltpu.VMEM((NTOK, 2 * D), BF), pltpu.SemaphoreType.DMA],
-        ins=[VMEM, HBM],
-    )(msg, both_all)
+        ins=[VMEM, VMEM, HBM],
+    )(msg, recv_b[:, FB:SENT_B], both_all)
     recv_a = lax.all_to_all(send_a.reshape(NE, 8, SENT_A), "expert", 0, 0, tiled=True)
     to_sum, to_send = call(
         experts_kernel,

time: 223 us -> 223 us (level)
  no operation moved by 1% of the time
where the time goes in v5:
time: 223 us
  blocking collectives  159 us (71%)
  Pallas kernels  19.2 us (9%)
  waiting for transfers between devices  15.5 us (7%)
  between operations  13.2 us (6%)
  starting transfers between devices  12.3 us (6%)
  local copies, waits for them, and re-layouts  3.27 us (1%)
    all_to_all x1, blocking collectives, per_device(): lax.all_to_all(send_a.reshape(NE, 8, SENT_A), 'expert', 0, 0, tiled=True)  50 us
    all_to_all x1, blocking collectives, per_device(): lax.all_to_all(to_send.reshape(NE, 8, BACK_A), 'expert', 0, 0, tiled=True)  40.8 us
    all_to_all x1, blocking collectives, per_device(): lax.all_to_all(send_b.reshape(NE, 8, SENT_B), 'expert', 0, 0, tiled=True)  32.7 us
    all_to_all x1, blocking collectives, per_device(): msg = lax.all_to_all(msg, 'tensor', 0, 0, tiled=True).reshape(NTOK, lanes)  20.6 us
    all_to_all x1, blocking collectives, per_device(): lax.all_to_all(last.reshape(NT, 8, LAST_PACKED), 'tensor', 0, 0, tiled=True)  15.1 us
    all_to_all x1, waiting for transfers between devices, per_device(): lax.all_to_all(summed.reshape(NE, 8, RB), 'expert', 0, 0, tiled=True)  12.3 us
    all_to_all x1, starting transfers between devices, per_device(): lax.all_to_all(summed.reshape(NE, 8, RB), 'expert', 0, 0, tiled=True)  12.2 us
    pallas_call x1, Pallas kernels, per_device(): call(experts_kernel, (shape(NT, ROWS, RB), shape(ROWS, BACK_A)), 'experts...  10.5 us
  transfers between devices with their start and end apart: 4, of which 2 were waited for; matrix products, arithmetic and copies ran while one was open for 0% of the time, Pallas kernels for 2%

profile of v5, /device:TPU:1, one launch (start us, length us, event | category | flops | bytes accessed | tf_op | source)
XLA Modules:
  0.0 222.7 jit_solution(11093088579678768434)
XLA Ops:
  6.5 1.8 start.1
  8.3 0.0 all-gather.3.cloned.1.call-update
  8.4 0.0 all-gather.5.cloned.1.call-start
  8.4 20.6 %all_to_all.30 = bf16[8,16,896]{2,1,0:T(8,128)(2,1)S(1)} all-to-all(bf16[8,16,896]{2,1,0:T(8,128)(2,1)} %get-tuple-element.11), channel_id=1, replica_groups=mesh['tensor'=8,'expert'=64] {'tensor'}, dimensions={0} | all-to-all | bytes 458752 | tf_op jit(solution)/shard_map/all_to_all | solution.py:486
  29.0 0.9 pack_b.1
  30.0 32.7 %all_to_all.31 = bf16[64,8,640]{2,1,0:T(8,128)(2,1)S(1)} all-to-all(bf16[64,8,640]{2,1,0:T(8,128)(2,1)S(1)} %bitcast.20), channel_id=1, replica_groups=mesh['tensor'=8,'expert'=64] {'expert'}, dimensions={0} | all-to-all | bytes 1310720 | tf_op jit(solution)/shard_map/all_to_all | solution.py:488
  62.6 1.0 unpack_b.1
  63.7 0.0 reduce-scatter.2.cloned.1.call-start
  63.7 0.0 all-gather.3.cloned.1.call-done.x_in
  63.8 1.3 copy-done
  65.1 2.0 pack_a.1
  67.1 0.7 copy-done.1
  67.8 50.0 %all_to_all.32 = bf16[64,8,1792]{2,1,0:T(8,128)(2,1)} all-to-all(bf16[64,8,1792]{2,1,0:T(8,128)(2,1)S(1)} %bitcast.21), channel_id=1, replica_groups=mesh['tensor'=8,'expert'=64] {'expert'}, dimensions={0} | all-to-all | bytes 3670016 | tf_op jit(solution)/shard_map/all_to_all | solution.py:500
  117.8 3.2 %all-gather.5.cloned.1.call-done.b_in = bf16[4608,512]{1,0:T(8,128)(2,1)} async-done(((bf16[576,512]{1,0:T(8,128)(2,1)}), bf16[4608,512]{1,0:T(8,128)(2,1)}) %all-gather.5.cloned.1.call-update) | async-done | bytes 4718608 | tf_op jit(solution)/shard_map/all_gather | solution.py:491
  121.0 10.5 %experts.1 = (bf16[8,512,256]{2,1,0:T(8,128)(2,1)}, bf16[512,1152]{1,0:T(8,128)(2,1)}) custom-call(bf16[512,1792]{1,0:T(8,128)(2,1)} %bitcast.24, bf16[4608,512]{1,0:T(8,128)(2,1)} %all-gather.5.cloned.1.call-done.b_in, f32[640,128]{1,0:T(8,128)} %copy-done.1, bf16[2,96,2560]{2,1,0:T(8,128)(2,1)} %wg_in.1, bf16[2,96,2560]{2,1,0:T(8,128)(2,1)} %wu_in.1, ...), custom_call_target="tpu_custom_call" | custom-call | flops 3145728000 | bytes 13000000 | tf_op jit(solution)/shard_map/experts/pallas_call | solution.py:501
  131.6 0.0 reduce-scatter.2.cloned.1.call-update
  131.6 1.2 copy-done.2
  132.8 40.8 %all_to_all.33 = bf16[64,8,1152]{2,1,0:T(8,128)(2,1)S(1)} all-to-all(bf16[64,8,1152]{2,1,0:T(8,128)(2,1)S(1)} %bitcast.25), channel_id=1, replica_groups=mesh['tensor'=8,'expert'=64] {'expert'}, dimensions={0} | all-to-all | bytes 2359296 | tf_op jit(solution)/shard_map/all_to_all | solution.py:526
  173.6 12.2 %all-to-all-start.3 = ((bf16[64,8,256]{2,1,0:T(8,128)(2,1)}), bf16[64,8,256]{2,1,0:T(8,128)(2,1)S(1)}, u32[]{:S(2)}, u32[]{:S(2)}) async-start(bf16[64,8,256]{2,1,0:T(8,128)(2,1)} %bitcast.26), calls=%async_computation.4 | async-start | bytes 524288 | tf_op jit(solution)/shard_map/all_to_all | solution.py:527
  185.8 0.9 combine_a.1.a_ref
  186.7 12.3 %all-to-all-done.3 = bf16[64,8,256]{2,1,0:T(8,128)(2,1)S(1)} async-done(((bf16[64,8,256]{2,1,0:T(8,128)(2,1)}), bf16[64,8,256]{2,1,0:T(8,128)(2,1)S(1)}, u32[]{:S(2)}, u32[]{:S(2)}) %all-to-all-start.3) | async-done | bytes 262176 | tf_op jit(solution)/shard_map/all_to_all | solution.py:527
  199.0 1.4 combine_b.1
  200.4 15.1 %all_to_all.34.in_ref = bf16[8,8,1920]{2,1,0:T(8,128)(2,1)S(1)} all-to-all(bf16[8,8,1920]{2,1,0:T(8,128)(2,1)S(1)} %bitcast.23), channel_id=1, replica_groups=mesh['tensor'=8,'expert'=64] {'tensor'}, dimensions={0} | all-to-all | bytes 491520 | tf_op jit(solution)/shard_map/all_to_all | solution.py:539
  215.5 0.7 finish.1
  (7 shorter events, 0.0 us)
Async XLA Ops:
  6.5 57.2 %all-gather.3.cloned.1.call-start = ((), (), s32[]{:S(2)}) async-start(), calls=%async_computation.7 | async-start | bytes 1474560 | tf_op jit(solution)/shard_map/all_gather | solution.py:485
  8.4 112.7 %all-gather.5.cloned.1.call-start = ((), (), s32[]{:S(2)}) async-start(), calls=%async_computation.8 | async-start | bytes 5308416 | tf_op jit(solution)/shard_map/all_gather | solution.py:491
  63.7 109.9 %reduce-scatter.2.cloned.1.call-start = ((), (), s32[]{:S(2)}) async-start(), calls=%async_computation.9 | async-start | bytes 2359296 | tf_op jit(solution)/shard_map/reduce_scatter | solution.py:525
  63.8 1.3 copy-start
  67.1 0.7 copy-start.1
  131.6 1.3 copy-start.2
  173.6 25.4 %all-to-all-start.3 = ((bf16[64,8,256]{2,1,0:T(8,128)(2,1)}), bf16[64,8,256]{2,1,0:T(8,128)(2,1)S(1)}, u32[]{:S(2)}, u32[]{:S(2)}) async-start(bf16[64,8,256]{2,1,0:T(8,128)(2,1)} %bitcast.26), calls=%async_computation.4 | async-start | bytes 524288 | tf_op jit(solution)/shard_map/all_to_all | solution.py:527
Sparse Core Ops, SparseCore 0:
  9.4 43.6 all-gather.2
  63.8 57.1 all-gather.4
  131.7 39.7 reduce-scatter.1

commit v6 on v5

--- a/solution.py
+++ b/solution.py
@@ -20,10 +20,11 @@
 FB = (D - FA) // 4
 LA = 1536
 LB = (D - LA) // 4
+FOURTH = [D * (t // 4) + LA + LB * (t % 4) + 128 for t in range(8)]
 META = 128
-SENT_A = 2 * FA + 2 * 2 * LA // 8
+SENT_A = 2 * FA + 2 * 2 * LA // 8 + 128
 SENT_B = FB + 128
-GATHERED = ROWS + NE
+GATHERED = ROWS + 48
 RA = 1024
 RB = 256
 BACK_A = RA + 128
@@ -113,13 +114,13 @@
     sub = row & 7
     main = jnp.where(spread == sub, 1.0, 0.0).astype(BF)
     left = jnp.where(spread == 8 + (sub >> 2), 1.0, 0.0).astype(BF)
-    return main, left
+    return main, left, mask(spread == 9)
 
 
 def pack_b_kernel(msg_ref, out_ref):
     meta = msg_ref[:, FB + LB : FB + LB + META]
     pos, ids = positions(meta)
-    main, left = one_hots(pos)
+    main, left, _ = one_hots(pos)
     out_ref[:, 0:FB] = dot(main, msg_ref[:, 0:FB]).astype(BF)
     row = iota((ROWS, 128), 0)
     sub = row & 7
@@ -144,12 +145,16 @@
 
 def unpack_b_kernel(in_ref, out_ref):
     out_ref[0:ROWS, :] = in_ref[:, 0:FB]
-    turn = perm(False)[0:128]
+    turn = perm(False)[0:96]
     for h in range(2):
         turned = dot(turn, in_ref[256 * h : 256 * (h + 1), FB : FB + 128]).astype(BF)
-        for r in range(4):
-            low = ROWS + 32 * h
-            out_ref[low : low + 32, 128 * r : 128 * (r + 1)] = turned[32 * r : 32 * (r + 1)]
+        for r in range(3):
+            for j in range(2):
+                place = 64 * r + 32 * h + 16 * j
+                low, tile = ROWS + place % 48, place // 48
+                out_ref[low : low + 16, 128 * tile : 128 * (tile + 1)] = turned[
+                    32 * r + 16 * j : 32 * r + 16 * (j + 1)
+                ]
 
 
 def gates_as_columns(tile_ref, gate_ref):
@@ -176,7 +181,7 @@
     copy.start()
     gates_as_columns(tile_ref, gate_ref)
     pos, _ = positions(msg_ref[:, FB + LB : FB + LB + META])
-    main, left = one_hots(pos)
+    main, left, last = one_hots(pos)
     sub4 = iota((ROWS, 128), 0) & 3
     copy.wait()
     for part in range(2):
@@ -189,6 +194,12 @@
                 out = jnp.where(sub4 == k, spread[:, 128 * k : 128 * (k + 1)], out)
             low = 2 * FA + 128 * (part * (LA // 512) + q)
             out_ref[:, low : low + 128] = out.astype(BF)
+    sub = iota((ROWS, 128), 0) & 7
+    out = jnp.zeros((ROWS, 128), F32)
+    for r in range(8):
+        low = FOURTH[r]
+        out = jnp.where(sub == r, dot(last, x_ref[:, low : low + 128]), out)
+    out_ref[:, SENT_A - 128 : SENT_A] = out.astype(BF)
 
 
 def perm(inverse):
@@ -258,7 +269,7 @@
     )
     main_copies = fetch(a_in, a_ref, [(every, pl.ds(FA * i, FA)) for i in range(2)]) + fetch_weights(0)
     b_copies = [
-        fetch(b_in, b_ref, [pl.ds(GATHERED * u + 288 * i, 288) for u in (t, t + 4) for i in range(2)])
+        fetch(b_in, b_ref, [pl.ds(GATHERED * u + 272 * i, 272 + 16 * i) for u in (t, t + 4) for i in range(2)])
         + fetch_weights(FA + FB * t)
         for t in range(4)
     ]
@@ -276,6 +287,11 @@
                     left_ref[low : low + 32, base + 128 * k : base + 128 * (k + 1)] = turned[
                         32 * (4 * s + k) : 32 * (4 * s + k + 1), 128 * q : 128 * (q + 1)
                     ]
+        for r in range(8):
+            low = 64 + 32 * h
+            left_ref[low : low + 32, FOURTH[r] : FOURTH[r] + 128] = turned[
+                32 * r : 32 * (r + 1), 4 * LA // 8 : 4 * LA // 8 + 128
+            ]
     arrive(main_copies)
 
     def block(ref, low):
@@ -304,10 +320,14 @@
         back_proj = back_proj + dot_t(b_ref[y0 : y0 + ROWS, :], block(wd_ref, low))
         for base, start in ((0, x0), (D, y0)):
             low = base + LA + LB * t
-            for s in range(2):
-                left_ref[64 * s : 64 * s + 64, low : low + LB] = b_ref[
-                    start + ROWS : start + GATHERED, LB * s : LB * (s + 1)
-                ]
+            for r in range(3):
+                for j in range(4):
+                    place = 64 * r + 16 * j
+                    src, tile = start + ROWS + place % 48, place // 48
+                    dst, col = 64 * (r // 2) + 16 * j, low + 128 * (r % 2)
+                    left_ref[dst : dst + 16, col : col + 128] = b_ref[
+                        src : src + 16, 128 * tile : 128 * (tile + 1)
+                    ]
         if FA + FB * (t + 1) <= LA:
             left_sums = add_left(left_sums, FA + FB * t)
     arrive(g_copies)

time: 223 us -> 222 us (level)
  waiting for transfers between devices: 15.5 us -> 12.3 us
    all_gather x1, waiting for transfers between devices: 3.21 us -> 0.01 us  [per_device(): all_b = lax.all_gather(own_b, 'tensor', axis=0, tiled=True)]
    all_to_all x1, blocking collectives: 50 us -> 52.7 us  [per_device(): lax.all_to_all(send_a.reshape(NE, 8, SENT_A), 'expert', 0, 0, tiled=True)]
  transfers between devices with their start and end apart: 4 -> 4, of which waited for: 2 -> 1; matrix products, arithmetic and copies ran while one was open for 0% -> 0% of each run, Pallas kernels for 2% -> 2%
where the time goes in v6:
time: 222 us; the launch traced here: 221 us
  blocking collectives  161 us (73%)
  Pallas kernels  19.6 us (9%)
  between operations  13.2 us (6%)
  starting transfers between devices  12.3 us (6%)
  waiting for transfers between devices  12.3 us (6%)
  local copies, waits for them, and re-layouts  3.27 us (1%)
    all_to_all x1, blocking collectives, per_device(): lax.all_to_all(send_a.reshape(NE, 8, SENT_A), 'expert', 0, 0, tiled=True)  52.7 us
    all_to_all x1, blocking collectives, per_device(): lax.all_to_all(to_send.reshape(NE, 8, BACK_A), 'expert', 0, 0, tiled=True)  40 us
    all_to_all x1, blocking collectives, per_device(): lax.all_to_all(send_b.reshape(NE, 8, SENT_B), 'expert', 0, 0, tiled=True)  32.7 us
    all_to_all x1, blocking collectives, per_device(): msg = lax.all_to_all(msg, 'tensor', 0, 0, tiled=True).reshape(NTOK, lanes)  20.6 us
    all_to_all x1, blocking collectives, per_device(): lax.all_to_all(last.reshape(NT, 8, LAST_PACKED), 'tensor', 0, 0, tiled=True)  14.7 us
    all_to_all x1, waiting for transfers between devices, per_device(): lax.all_to_all(summed.reshape(NE, 8, RB), 'expert', 0, 0, tiled=True)  12.3 us
    all_to_all x1, starting transfers between devices, per_device(): lax.all_to_all(summed.reshape(NE, 8, RB), 'expert', 0, 0, tiled=True)  12.2 us
    pallas_call x1, Pallas kernels, per_device(): call(experts_kernel, (shape(NT, ROWS, RB), shape(ROWS, BACK_A)), 'experts...  10.6 us
  transfers between devices with their start and end apart: 4, of which 1 were waited for; matrix products, arithmetic and copies ran while one was open for 0% of the time, Pallas kernels for 2%

profile of v6, /device:TPU:1, one launch (start us, length us, event | category | flops | bytes accessed | tf_op | source)
XLA Modules:
  0.0 221.3 jit_solution(16106238747428875271)
XLA Ops:
  6.5 1.8 start.1
  8.3 0.0 all-gather.3.cloned.1.call-update
  8.4 0.0 all-gather.5.cloned.1.call-start
  8.4 20.6 %all_to_all.30 = bf16[8,16,896]{2,1,0:T(8,128)(2,1)S(1)} all-to-all(bf16[8,16,896]{2,1,0:T(8,128)(2,1)} %get-tuple-element.11), channel_id=1, replica_groups=mesh['tensor'=8,'expert'=64] {'tensor'}, dimensions={0} | all-to-all | bytes 458752 | tf_op jit(solution)/shard_map/all_to_all | solution.py:506
  29.0 0.9 pack_b.1
  30.0 32.7 %all_to_all.31 = bf16[64,8,640]{2,1,0:T(8,128)(2,1)S(1)} all-to-all(bf16[64,8,640]{2,1,0:T(8,128)(2,1)S(1)} %bitcast.20), channel_id=1, replica_groups=mesh['tensor'=8,'expert'=64] {'expert'}, dimensions={0} | all-to-all | bytes 1310720 | tf_op jit(solution)/shard_map/all_to_all | solution.py:508
  62.6 1.0 unpack_b.1
  63.6 0.0 all-gather.5.cloned.1.call-update
  63.7 0.0 reduce-scatter.2.cloned.1.call-start
  63.7 0.0 all-gather.3.cloned.1.call-done.x_in
  63.8 1.3 copy-done
  65.1 2.3 %pack_a.1 = (bf16[512,1920]{1,0:T(8,128)(2,1)S(1)}, f32[640,128]{1,0:T(8,128)S(1)}) custom-call(bf16[128,896]{1,0:T(8,128)(2,1)S(1)} %bitcast.15, bf16[512,128]{1,0:T(8,128)(2,1)S(1)} %slice.4.tile_ref, bf16[128,5120]{1,0:T(8,128)(2,1)S(1)} %copy-done), custom_call_target="tpu_custom_call" | custom-call | flops 536870912 | tf_op jit(solution)/shard_map/pack_a/pallas_call | solution.py:512
  67.3 0.7 copy-done.1
  68.1 52.7 %all_to_all.32 = bf16[64,8,1920]{2,1,0:T(8,128)(2,1)} all-to-all(bf16[64,8,1920]{2,1,0:T(8,128)(2,1)S(1)} %bitcast.21), channel_id=1, replica_groups=mesh['tensor'=8,'expert'=64] {'expert'}, dimensions={0} | all-to-all | bytes 3932160 | tf_op jit(solution)/shard_map/all_to_all | solution.py:520
  120.7 10.6 %experts.1 = (bf16[8,512,256]{2,1,0:T(8,128)(2,1)}, bf16[512,1152]{1,0:T(8,128)(2,1)}) custom-call(bf16[512,1920]{1,0:T(8,128)(2,1)} %bitcast.24, bf16[4480,512]{1,0:T(8,128)(2,1)} %all-gather.5.cloned.1.call-done.b_in, f32[640,128]{1,0:T(8,128)} %copy-done.1, bf16[2,96,2560]{2,1,0:T(8,128)(2,1)} %wg_in.1, bf16[2,96,2560]{2,1,0:T(8,128)(2,1)} %wu_in.1, ...), custom_call_target="tpu_custom_call" | custom-call | flops 3145728000 | bytes 13000000 | tf_op jit(solution)/shard_map/experts/pallas_call | solution.py:521
  131.4 0.0 reduce-scatter.2.cloned.1.call-update
  131.4 1.2 copy-done.2
  132.6 40.0 %all_to_all.33 = bf16[64,8,1152]{2,1,0:T(8,128)(2,1)S(1)} all-to-all(bf16[64,8,1152]{2,1,0:T(8,128)(2,1)S(1)} %bitcast.25), channel_id=1, replica_groups=mesh['tensor'=8,'expert'=64] {'expert'}, dimensions={0} | all-to-all | bytes 2359296 | tf_op jit(solution)/shard_map/all_to_all | solution.py:546
  172.6 12.2 %all-to-all-start.3 = ((bf16[64,8,256]{2,1,0:T(8,128)(2,1)}), bf16[64,8,256]{2,1,0:T(8,128)(2,1)S(1)}, u32[]{:S(2)}, u32[]{:S(2)}) async-start(bf16[64,8,256]{2,1,0:T(8,128)(2,1)} %bitcast.26), calls=%async_computation.4 | async-start | bytes 524288 | tf_op jit(solution)/shard_map/all_to_all | solution.py:547
  184.8 0.9 combine_a.1.a_ref
  185.7 12.3 %all-to-all-done.3 = bf16[64,8,256]{2,1,0:T(8,128)(2,1)S(1)} async-done(((bf16[64,8,256]{2,1,0:T(8,128)(2,1)}), bf16[64,8,256]{2,1,0:T(8,128)(2,1)S(1)}, u32[]{:S(2)}, u32[]{:S(2)}) %all-to-all-start.3) | async-done | bytes 262176 | tf_op jit(solution)/shard_map/all_to_all | solution.py:547
  198.0 1.4 combine_b.1
  199.4 14.7 %all_to_all.34.in_ref = bf16[8,8,1920]{2,1,0:T(8,128)(2,1)S(1)} all-to-all(bf16[8,8,1920]{2,1,0:T(8,128)(2,1)S(1)} %bitcast.23), channel_id=1, replica_groups=mesh['tensor'=8,'expert'=64] {'tensor'}, dimensions={0} | all-to-all | bytes 491520 | tf_op jit(solution)/shard_map/all_to_all | solution.py:559
  214.1 0.7 finish.1
  (7 shorter events, 0.0 us)
Async XLA Ops:
  6.5 57.2 %all-gather.3.cloned.1.call-start = ((), (), s32[]{:S(2)}) async-start(), calls=%async_computation.7 | async-start | bytes 1474560 | tf_op jit(solution)/shard_map/all_gather | solution.py:505
  8.4 112.4 %all-gather.5.cloned.1.call-start = ((), (), s32[]{:S(2)}) async-start(), calls=%async_computation.8 | async-start | bytes 5160960 | tf_op jit(solution)/shard_map/all_gather | solution.py:511
  63.7 108.9 %reduce-scatter.2.cloned.1.call-start = ((), (), s32[]{:S(2)}) async-start(), calls=%async_computation.9 | async-start | bytes 2359296 | tf_op jit(solution)/shard_map/reduce_scatter | solution.py:545
  63.8 1.3 copy-start
  67.3 0.7 copy-start.1
  131.4 1.3 copy-start.2
  172.6 25.4 %all-to-all-start.3 = ((bf16[64,8,256]{2,1,0:T(8,128)(2,1)}), bf16[64,8,256]{2,1,0:T(8,128)(2,1)S(1)}, u32[]{:S(2)}, u32[]{:S(2)}) async-start(bf16[64,8,256]{2,1,0:T(8,128)(2,1)} %bitcast.26), calls=%async_computation.4 | async-start | bytes 524288 | tf_op jit(solution)/shard_map/all_to_all | solution.py:547
Sparse Core Ops, SparseCore 0:
  9.4 43.6 all-gather.2
  63.8 55.9 all-gather.4
  131.5 38.5 reduce-scatter.1

commit v7 on v6

--- a/solution.py
+++ b/solution.py
@@ -176,16 +176,32 @@
     gate_ref[ROWS : ROWS + 128, :] = rest
 
 
-def pack_a_kernel(msg_ref, tile_ref, x_in, out_ref, gate_ref, x_ref, sem):
-    copy = pltpu.make_async_copy(x_in, x_ref, sem)
-    copy.start()
+def pack_a_kernel(msg_ref, tile_ref, x_in, send_out, gate_out, x_ref, out_ref, gate_ref, sems, out_sems):
+    copies = []
+    for i in range(2 * D // 512):
+        part = (slice(None), pl.ds(512 * i, 512))
+        copies.append(pltpu.make_async_copy(x_in.at[part], x_ref.at[part], sems.at[i]))
+        copies[-1].start()
+    outs = []
+
+    def send(src, dst):
+        outs.append(pltpu.make_async_copy(src, dst, out_sems.at[len(outs)]))
+        outs[-1].start()
+
+    def send_lanes(low, width):
+        part = (slice(None), pl.ds(low, width))
+        send(out_ref.at[part], send_out.at[part])
+
     gates_as_columns(tile_ref, gate_ref)
+    send(gate_ref, gate_out)
     pos, _ = positions(msg_ref[:, FB + LB : FB + LB + META])
     main, left, last = one_hots(pos)
     sub4 = iota((ROWS, 128), 0) & 3
-    copy.wait()
+    for copy in copies:
+        copy.wait()
     for part in range(2):
         out_ref[:, part * FA : (part + 1) * FA] = dot(main, x_ref[:, part * D : part * D + FA]).astype(BF)
+        send_lanes(part * FA, FA)
         for q in range(LA // 512):
             low = part * D + 512 * q
             spread = dot(left, x_ref[:, low : low + 512])
@@ -200,6 +216,9 @@
         low = FOURTH[r]
         out = jnp.where(sub == r, dot(last, x_ref[:, low : low + 128]), out)
     out_ref[:, SENT_A - 128 : SENT_A] = out.astype(BF)
+    send_lanes(2 * FA, SENT_A - 2 * FA)
+    for copy in outs:
+        copy.wait()
 
 
 def perm(inverse):
@@ -514,8 +533,16 @@
         (shape(ROWS, SENT_A), shape(ROWS + 128, 128, dtype=F32)),
         "pack_a",
         flops=2 * ROWS * 128 * 4096,
-        scratch=[pltpu.VMEM((NTOK, 2 * D), BF), pltpu.SemaphoreType.DMA],
+        scratch=[
+            pltpu.VMEM((NTOK, 2 * D), BF),
+            pltpu.VMEM((ROWS, SENT_A), BF),
+            pltpu.VMEM((ROWS + 128, 128), F32),
+            pltpu.SemaphoreType.DMA((2 * D // 512,)),
+            pltpu.SemaphoreType.DMA((4,)),
+        ],
+        limit=LARGE,
         ins=[VMEM, VMEM, HBM],
+        outs=(HBM, HBM),
     )(msg, recv_b[:, FB:SENT_B], both_all)
     recv_a = lax.all_to_all(send_a.reshape(NE, 8, SENT_A), "expert", 0, 0, tiled=True)
     to_sum, to_send = call(

time: 222 us -> 222 us (level)
  Pallas kernels: 19.6 us -> 22.4 us
    pallas_call x1, Pallas kernels: 2.25 us -> 5.03 us  [per_device(): call(pack_a_kernel, (shape(ROWS, SENT_A), shape(ROWS + 128, 128, dtype=F3...]
  transfers between devices with their start and end apart: 4 -> 4, of which waited for: 1 -> 1; matrix products, arithmetic and copies ran while one was open for 0% -> 0% of each run, Pallas kernels for 2% -> 4%
where the time goes in v7:
time: 222 us; the launch traced here: 221 us
  blocking collectives  160 us (72%)
  Pallas kernels  22.4 us (10%)
  between operations  13.2 us (6%)
  waiting for transfers between devices  12.3 us (6%)
  starting transfers between devices  12.1 us (5%)
    all_to_all x1, blocking collectives, per_device(): lax.all_to_all(send_a.reshape(NE, 8, SENT_A), 'expert', 0, 0, tiled=True)  52.9 us
    all_to_all x1, blocking collectives, per_device(): lax.all_to_all(to_send.reshape(NE, 8, BACK_A), 'expert', 0, 0, tiled=True)  38.3 us
    all_to_all x1, blocking collectives, per_device(): lax.all_to_all(send_b.reshape(NE, 8, SENT_B), 'expert', 0, 0, tiled=True)  32.7 us
    all_to_all x1, blocking collectives, per_device(): msg = lax.all_to_all(msg, 'tensor', 0, 0, tiled=True).reshape(NTOK, lanes)  20.6 us
    all_to_all x1, blocking collectives, per_device(): lax.all_to_all(last.reshape(NT, 8, LAST_PACKED), 'tensor', 0, 0, tiled=True)  15.1 us
    all_to_all x1, waiting for transfers between devices, per_device(): lax.all_to_all(summed.reshape(NE, 8, RB), 'expert', 0, 0, tiled=True)  12.2 us
    all_to_all x1, starting transfers between devices, per_device(): lax.all_to_all(summed.reshape(NE, 8, RB), 'expert', 0, 0, tiled=True)  12 us
    pallas_call x1, Pallas kernels, per_device(): call(experts_kernel, (shape(NT, ROWS, RB), shape(ROWS, BACK_A)), 'experts...  10.6 us
  transfers between devices with their start and end apart: 4, of which 1 were waited for; matrix products, arithmetic and copies ran while one was open for 0% of the time, Pallas kernels for 4%

profile of v7, /device:TPU:1, one launch (start us, length us, event | category | flops | bytes accessed | tf_op | source)
XLA Modules:
  0.0 221.5 jit_solution(13871973874833929983)
XLA Ops:
  6.5 0.0 all-gather.3.cloned.1.call-start
  6.5 1.8 start.1
  8.3 0.0 all-gather.3.cloned.1.call-update
  8.4 0.0 all-gather.5.cloned.1.call-start
  8.4 20.6 %all_to_all.30 = bf16[8,16,896]{2,1,0:T(8,128)(2,1)S(1)} all-to-all(bf16[8,16,896]{2,1,0:T(8,128)(2,1)} %get-tuple-element.11), channel_id=1, replica_groups=mesh['tensor'=8,'expert'=64] {'tensor'}, dimensions={0} | all-to-all | bytes 458752 | tf_op jit(solution)/shard_map/all_to_all | solution.py:525
  29.0 0.9 pack_b.1
  30.0 32.7 %all_to_all.31 = bf16[64,8,640]{2,1,0:T(8,128)(2,1)S(1)} all-to-all(bf16[64,8,640]{2,1,0:T(8,128)(2,1)S(1)} %bitcast.20), channel_id=1, replica_groups=mesh['tensor'=8,'expert'=64] {'expert'}, dimensions={0} | all-to-all | bytes 1310720 | tf_op jit(solution)/shard_map/all_to_all | solution.py:527
  62.6 1.1 unpack_b.1
  63.7 0.0 all-gather.5.cloned.1.call-update
  63.7 0.0 reduce-scatter.2.cloned.1.call-start
  63.8 0.7 slice.4.tile_ref
  64.5 5.0 %pack_a.1 = (bf16[512,1920]{1,0:T(8,128)(2,1)}, f32[640,128]{1,0:T(8,128)}) custom-call(bf16[128,896]{1,0:T(8,128)(2,1)} %bitcast.15, bf16[512,128]{1,0:T(8,128)(2,1)} %slice.4.tile_ref, bf16[128,5120]{1,0:T(8,128)(2,1)} %all-gather.3.cloned.1.call-done.x_in), custom_call_target="tpu_custom_call" | custom-call | flops 536870912 | tf_op jit(solution)/shard_map/pack_a/pallas_call | solution.py:531
  69.5 52.9 %all_to_all.32 = bf16[64,8,1920]{2,1,0:T(8,128)(2,1)} all-to-all(bf16[64,8,1920]{2,1,0:T(8,128)(2,1)} %bitcast.24), channel_id=1, replica_groups=mesh['tensor'=8,'expert'=64] {'expert'}, dimensions={0} | all-to-all | bytes 3932160 | tf_op jit(solution)/shard_map/all_to_all | solution.py:547
  122.4 10.6 %experts.1 = (bf16[8,512,256]{2,1,0:T(8,128)(2,1)}, bf16[512,1152]{1,0:T(8,128)(2,1)}) custom-call(bf16[512,1920]{1,0:T(8,128)(2,1)} %bitcast.23, bf16[4480,512]{1,0:T(8,128)(2,1)} %all-gather.5.cloned.1.call-done.b_in, f32[640,128]{1,0:T(8,128)} %get-tuple-element.14.gates_in, bf16[2,96,2560]{2,1,0:T(8,128)(2,1)} %wg_in.1, bf16[2,96,2560]{2,1,0:T(8,128)(2,1)} %wu_in.1, ...), custom_call_target="tpu_custom_call" | custom-call | flops 3145728000 | bytes 13000000 | tf_op jit(solution)/shard_map/experts/pallas_call | solution.py:548
  133.0 0.0 copy-start.2
  133.0 0.0 reduce-scatter.2.cloned.1.call-update
  133.0 1.2 copy-done.2
  134.3 38.3 %all_to_all.33 = bf16[64,8,1152]{2,1,0:T(8,128)(2,1)S(1)} all-to-all(bf16[64,8,1152]{2,1,0:T(8,128)(2,1)S(1)} %bitcast.25), channel_id=1, replica_groups=mesh['tensor'=8,'expert'=64] {'expert'}, dimensions={0} | all-to-all | bytes 2359296 | tf_op jit(solution)/shard_map/all_to_all | solution.py:573
  172.6 12.0 %all-to-all-start.3 = ((bf16[64,8,256]{2,1,0:T(8,128)(2,1)}), bf16[64,8,256]{2,1,0:T(8,128)(2,1)S(1)}, u32[]{:S(2)}, u32[]{:S(2)}) async-start(bf16[64,8,256]{2,1,0:T(8,128)(2,1)} %bitcast.26), calls=%async_computation.4 | async-start | bytes 524288 | tf_op jit(solution)/shard_map/all_to_all | solution.py:574
  184.6 0.9 combine_a.1.a_ref
  185.5 12.2 %all-to-all-done.3 = bf16[64,8,256]{2,1,0:T(8,128)(2,1)S(1)} async-done(((bf16[64,8,256]{2,1,0:T(8,128)(2,1)}), bf16[64,8,256]{2,1,0:T(8,128)(2,1)S(1)}, u32[]{:S(2)}, u32[]{:S(2)}) %all-to-all-start.3) | async-done | bytes 262176 | tf_op jit(solution)/shard_map/all_to_all | solution.py:574
  197.8 1.4 combine_b.1
  199.2 15.1 %all_to_all.34.in_ref = bf16[8,8,1920]{2,1,0:T(8,128)(2,1)S(1)} all-to-all(bf16[8,8,1920]{2,1,0:T(8,128)(2,1)S(1)} %bitcast.22), channel_id=1, replica_groups=mesh['tensor'=8,'expert'=64] {'tensor'}, dimensions={0} | all-to-all | bytes 491520 | tf_op jit(solution)/shard_map/all_to_all | solution.py:586
  214.3 0.7 finish.1
  (7 shorter events, 0.0 us)
Async XLA Ops:
  6.5 57.9 %all-gather.3.cloned.1.call-start = ((), (), s32[]{:S(2)}) async-start(), calls=%async_computation.7 | async-start | bytes 1474560 | tf_op jit(solution)/shard_map/all_gather | solution.py:524
  8.4 114.0 %all-gather.5.cloned.1.call-start = ((), (), s32[]{:S(2)}) async-start(), calls=%async_computation.8 | async-start | bytes 5160960 | tf_op jit(solution)/shard_map/all_gather | solution.py:530
  29.0 34.7 %copy-start = (bf16[8,16,896]{2,1,0:T(8,128)(2,1)}, bf16[8,16,896]{2,1,0:T(8,128)(2,1)S(1)}, u32[]{:S(2)}) copy-start(bf16[8,16,896]{2,1,0:T(8,128)(2,1)S(1)} %all_to_all.30) | copy-start | bytes 688132
  63.7 108.9 %reduce-scatter.2.cloned.1.call-start = ((), (), s32[]{:S(2)}) async-start(), calls=%async_computation.9 | async-start | bytes 2359296 | tf_op jit(solution)/shard_map/reduce_scatter | solution.py:572
  133.0 1.3 copy-start.2
  133.0 51.6 %copy-start.1 = (bf16[8,16,896]{2,1,0:T(8,128)(2,1)S(1)}, bf16[8,16,896]{2,1,0:T(8,128)(2,1)}, u32[]{:S(2)}) copy-start(bf16[8,16,896]{2,1,0:T(8,128)(2,1)} %copy-done) | copy-start | bytes 688132
  172.6 25.2 %all-to-all-start.3 = ((bf16[64,8,256]{2,1,0:T(8,128)(2,1)}), bf16[64,8,256]{2,1,0:T(8,128)(2,1)S(1)}, u32[]{:S(2)}, u32[]{:S(2)}) async-start(bf16[64,8,256]{2,1,0:T(8,128)(2,1)} %bitcast.26), calls=%async_computation.4 | async-start | bytes 524288 | tf_op jit(solution)/shard_map/all_to_all | solution.py:574
Sparse Core Ops, SparseCore 0:
  9.4 43.6 all-gather.2
  63.9 55.9 all-gather.4
  133.2 37.2 reduce-scatter.1
